TPU v7x, 512 devices: a whole 4x4x16 slice. The times are simulated.
512 devices in a mesh: seq: 128 (over z, y, core), head: 4 (over x).
Axes of the slice: x: 4, y: 4, z: 16, core: 2. Of those that a mesh axis runs over, the one named last changes fastest.
Arguments:
- tile_rows: bfloat16 [65536, 768], P('seq'), may hold values from -16 to 16
- tissue_mask: int32 [65536], replicated, may hold values 0 or 1
- slide_lengths: int32 [8], replicated, may hold values from 1 to 16384, 65536 in all
- region_rows: bfloat16 [4096, 768], P('seq'), may hold values from -6 to 6
- parent_lists: int32 [4096, 16], P('seq'), may hold values from 0 to 65535, as said below
- child_counts: int32 [4096], P('seq'), may hold values from 0 to 16, as said below
- region_cotangent: bfloat16 [4096, 768], P('seq'), may hold values from -6 to 6
- w_query: bfloat16 [768, 768], P(None, 'head'), may hold values from -0.21875 to 0.21875
- w_key: bfloat16 [768, 768], P(None, 'head'), may hold values from -0.21875 to 0.21875
- w_value: bfloat16 [768, 768], P(None, 'head'), may hold values from -0.21875 to 0.21875
- w_output: bfloat16 [768, 768], P('head'), may hold values from -0.21875 to 0.21875
- w_cross_query: bfloat16 [768, 768], P(None, 'head'), may hold values from -0.21875 to 0.21875
- w_cross_output: bfloat16 [768, 768], P('head'), may hold values from -0.21875 to 0.21875
Outputs:
- tile_output: bfloat16 [65536, 768], P('seq', 'head')
- region_output: bfloat16 [4096, 768], P('seq', 'head')
- value_grad: bfloat16 [65536, 768], P('seq', 'head')
Inputs may be any that keep to these rules, and one draw needn't show every extreme that they name: `parent_lists`: every entry of row r lies within 128 positions of the tiles 512 * (r // 32) to 512 * (r // 32 + 1) - 1; only the first child_counts[r] entries are children, later entries are ignored. `child_counts`: the first and the last region of every block of 32 regions have 16 children.
All inputs are finite; a program needn't handle non-finite values.
Results may differ from a plain program's by a relative error of at most 0.019.
Values may be sent and summed in bfloat16 or wider, within the bound.
A program may use at most 64 MiB of HBM per device.

v0:
```python
import jax
import jax.numpy as jnp
from jax import lax
from jax.sharding import PartitionSpec as P

HD = 64


def extended_2(cells, sides, width):
    for axis, dim in sides:
        count = lax.axis_size(axis)
        ends = count - 1
        head = lax.slice_in_dim(cells, 0, width, axis=dim)
        tail = lax.slice_in_dim(cells, cells.shape[dim] - width, cells.shape[dim], axis=dim)
        cells = jnp.concatenate(
            [
                lax.ppermute(tail, axis, [(i, (i + 1) % count) for i in range(ends)]),
                cells,
                lax.ppermute(head, axis, [((i + 1) % count, i) for i in range(ends)]),
            ],
            axis=dim,
        )
    return cells


def shifted(array, axis, by):
    peers = lax.axis_size(axis)
    pairs = [(i, i + by) for i in range(peers) if 0 <= i + by < peers]
    return lax.ppermute(array, axis, pairs)


def project(rows, weight):
    return jnp.dot(rows, weight, preferred_element_type=jnp.float32).astype(jnp.bfloat16)


def body(
    tile_rows,
    tissue_mask,
    slide_lengths,
    region_rows,
    parent_lists,
    child_counts,
    region_cotangent,
    w_query,
    w_key,
    w_value,
    w_output,
    w_cross_query,
    w_cross_output,
):
    rows_dev, model_width = tile_rows.shape
    head_cols = w_query.shape[1]
    local_heads = head_cols // HD
    groups = lax.axis_size("seq")
    stride_rows = rows_dev // groups
    seq_index = lax.axis_index("seq")
    head_index = lax.axis_index("head")
    score_scale = HD ** (-0.5)
    key_block = project(tile_rows, w_key)
    value_block = project(tile_rows, w_value)
    moved_rows = lax.all_to_all(
        tile_rows.reshape(stride_rows, groups, model_width),
        "seq",
        split_axis=1,
        concat_axis=0,
        tiled=True,
    )
    moved_rows = moved_rows.reshape(rows_dev, model_width)
    query_class = project(moved_rows, w_query)
    key_class = project(moved_rows, w_key)
    value_class = project(moved_rows, w_value)
    order_rows = jnp.arange(rows_dev, dtype=jnp.int32)
    positions = seq_index + groups * order_rows
    slide_ends = jnp.cumsum(slide_lengths)
    slide_ids = jnp.sum((positions[:, None] >= slide_ends[None, :]).astype(jnp.int32), axis=1)
    tissue_rows = lax.dynamic_slice_in_dim(tissue_mask.reshape(rows_dev, groups), seq_index, 1, 1)[
        :, 0
    ]
    offsets = order_rows[:, None] - order_rows[None, :]
    anchor_mask = (slide_ids[:, None] == slide_ids[None, :]) & (
        (tissue_rows[None, :] == 1) | (offsets == 0)
    )
    attended_heads = []
    for local_head in range(local_heads):
        global_head = head_index * local_heads + local_head
        dilation = jnp.left_shift(jnp.int32(1), global_head % 4)
        allowed = anchor_mask & (jnp.mod(offsets, dilation) == 0)
        query_head = query_class[:, local_head * HD : (local_head + 1) * HD]
        key_head = key_class[:, local_head * HD : (local_head + 1) * HD]
        value_head = value_class[:, local_head * HD : (local_head + 1) * HD]
        scores = (
            lax.dot_general(
                query_head, key_head, (((1,), (1,)), ((), ())), preferred_element_type=jnp.float32
            )
            * score_scale
        )
        highest = jnp.max(jnp.where(allowed, scores, -1e30), axis=1, keepdims=True)
        expon = jnp.where(allowed, jnp.exp(scores - highest), 0.0)
        weights = (expon / jnp.sum(expon, axis=1, keepdims=True)).astype(jnp.bfloat16)
        attended_heads.append(
            jnp.dot(weights, value_head, preferred_element_type=jnp.float32).astype(jnp.bfloat16)
        )
    attended_class = jnp.concatenate(attended_heads, axis=1)
    returned = lax.all_to_all(
        attended_class.reshape(rows_dev, 1, head_cols),
        "seq",
        split_axis=0,
        concat_axis=1,
        tiled=True,
    )
    attended = returned.reshape(rows_dev, head_cols)
    partial_sums = jnp.dot(attended, w_output, preferred_element_type=jnp.float32)
    tile_output = lax.psum_scatter(
        partial_sums.astype(jnp.bfloat16), "head", scatter_dimension=1, tiled=True
    )
    region_count = region_rows.shape[0]
    kid_slots = parent_lists.shape[1]
    reach = rows_dev // 4
    paired = jnp.concatenate([key_block, value_block], axis=1)
    extended = extended_2(paired, (("seq", 0),), reach)
    slot_rows = parent_lists - (seq_index * rows_dev - reach)
    picked = jnp.take(extended, slot_rows.reshape(-1), axis=0).reshape(
        region_count, kid_slots, 2 * head_cols
    )
    child_key = picked[:, :, :head_cols].reshape(region_count, kid_slots, local_heads, HD)
    child_value = picked[:, :, head_cols:].reshape(region_count, kid_slots, local_heads, HD)
    cross_query = project(region_rows, w_cross_query).reshape(region_count, local_heads, HD)
    own_key = project(region_rows, w_key).reshape(region_count, local_heads, HD)
    own_value = project(region_rows, w_value).reshape(region_count, local_heads, HD)
    own_score = (
        jnp.einsum("rhd,rhd->rh", cross_query, own_key, preferred_element_type=jnp.float32)[
            :, :, None
        ]
        * score_scale
    )
    child_score = (
        jnp.einsum("rhd,rkhd->rhk", cross_query, child_key, preferred_element_type=jnp.float32)
        * score_scale
    )
    scores = jnp.concatenate([own_score, child_score], axis=2)
    valid = jnp.arange(kid_slots, dtype=jnp.int32)[None, :] < child_counts[:, None]
    valid = jnp.concatenate([jnp.ones((region_count, 1), bool), valid], axis=1)[:, None, :]
    highest = jnp.max(jnp.where(valid, scores, -1e30), axis=2, keepdims=True)
    expon = jnp.where(valid, jnp.exp(scores - highest), 0.0)
    cross_weights = (expon / jnp.sum(expon, axis=2, keepdims=True)).astype(jnp.bfloat16)
    own_weight = cross_weights[:, :, 0:1].astype(jnp.float32)
    child_weight = cross_weights[:, :, 1:]
    mixed = own_weight * own_value.astype(jnp.float32) + jnp.einsum(
        "rhk,rkhd->rhd", child_weight, child_value, preferred_element_type=jnp.float32
    )
    cross_attended = mixed.reshape(region_count, head_cols).astype(jnp.bfloat16)
    region_terms = jnp.dot(cross_attended, w_cross_output, preferred_element_type=jnp.float32)
    region_output = lax.psum_scatter(
        region_terms.astype(jnp.bfloat16), "head", scatter_dimension=1, tiled=True
    )
    back_signal = jnp.dot(
        region_cotangent, jnp.transpose(w_cross_output), preferred_element_type=jnp.float32
    )
    back_signal = back_signal.reshape(region_count, local_heads, HD)
    child_weight_f = jnp.transpose(child_weight.astype(jnp.float32), (0, 2, 1))
    grad_terms = child_weight_f[:, :, :, None] * back_signal[:, None, :, :]
    grad_extended = jnp.zeros((rows_dev + 2 * reach, head_cols), jnp.float32)
    grad_extended = grad_extended.at[slot_rows.reshape(-1)].add(
        grad_terms.reshape(region_count * kid_slots, head_cols)
    )
    from_next = shifted(grad_extended[:reach].astype(jnp.bfloat16), "seq", -1).astype(jnp.float32)
    from_prior = shifted(grad_extended[rows_dev + reach :].astype(jnp.bfloat16), "seq", 1).astype(
        jnp.float32
    )
    own_grad = grad_extended[reach : reach + rows_dev]
    own_grad = own_grad.at[:reach].add(from_prior)
    own_grad = own_grad.at[rows_dev - reach :].add(from_next)
    return (tile_output, region_output, own_grad.astype(jnp.bfloat16))


def solution(mesh):
    in_specs = (
        P("seq", None),
        P(),
        P(),
        P("seq", None),
        P("seq", None),
        P("seq"),
        P("seq", None),
        P(None, "head"),
        P(None, "head"),
        P(None, "head"),
        P("head", None),
        P(None, "head"),
        P("head", None),
    )
    out_specs = (P("seq", "head"), P("seq", "head"), P("seq", "head"))
    return jax.shard_map(body, mesh=mesh, in_specs=in_specs, out_specs=out_specs, check_vma=False)
```

profile of v0, /device:TPU:1, one launch (start us, length us, event | category | flops | bytes accessed | tf_op | source)
XLA Modules:
  0.0 260.8 jit_solution(9927489752299495378)
XLA Ops:
  7.2 1.7 convolution_convert_fusion.1
  8.9 0.4 convolution_convert_fusion.2
  9.4 4.6 %collective-permute-start = (bf16[128,384]{0,1:T(8,128)(2,1)S(1)}, bf16[128,384]{0,1:T(8,128)(2,1)S(1)}, u32[]{:S(2)}, u32[]{:S(2)}) collective-permute-start(bf16[128,384]{0,1:T(8,128)(2,1)S(1)} %get-tuple-element.51), channel_id=1, source_target_pairs={{0,4},{4,8},{8,12},{12,16},{16,20},{20,24},{24,28},{28,32},{32,36}... | collective-permute-start | bytes 294920 | tf_op jit(solution)/shard_map/ppermute | solution.py:17
  14.0 5.5 %collective-permute-start.1 = (bf16[128,384]{0,1:T(8,128)(2,1)S(1)}, bf16[128,384]{0,1:T(8,128)(2,1)S(1)}, u32[]{:S(2)}, u32[]{:S(2)}) collective-permute-start(bf16[128,384]{0,1:T(8,128)(2,1)S(1)} %get-tuple-element.52), channel_id=1, source_target_pairs={{4,0},{8,4},{12,8},{16,12},{20,16},{24,20},{28,24},{32,28},{36,32}... | collective-permute-start | bytes 294920 | tf_op jit(solution)/shard_map/ppermute | solution.py:19
  19.5 1.5 copy.48
  21.0 16.9 %all-to-all-start = ((bf16[4,128,768]{2,0,1:T(4,128)(2,1)}), bf16[4,128,768]{2,0,1:T(4,128)(2,1)S(1)}, u32[]{:S(2)}, u32[]{:S(2)}) async-start(bf16[4,128,768]{2,0,1:T(4,128)(2,1)} %copy.48), calls=%async_computation | async-start | bytes 1572864 | tf_op jit(solution)/shard_map/all_to_all | solution.py:61
  37.9 0.2 convolution_convert_fusion.11
  38.1 0.2 convolution_convert_fusion.12
  38.3 0.1 reshape.197
  38.5 0.1 reshape.228
  38.6 0.2 reduce-window.8
  39.2 0.1 fusion.49
  39.4 0.2 fusion
  39.6 0.1 reshape.203
  39.8 0.2 fusion.34
  40.2 0.3 copy.53
  40.5 2.1 gather_fusion
  42.7 0.1 broadcast_select_fusion
  42.8 0.1 fusion.59
  43.0 0.1 reshape.200
  43.1 0.3 fusion.30
  43.7 35.6 %all-to-all-done = bf16[4,128,768]{2,0,1:T(4,128)(2,1)S(1)} async-done(((bf16[4,128,768]{2,0,1:T(4,128)(2,1)}), bf16[4,128,768]{2,0,1:T(4,128)(2,1)S(1)}, u32[]{:S(2)}, u32[]{:S(2)}) %all-to-all-start) | async-done | bytes 786464 | tf_op jit(solution)/shard_map/all_to_all | solution.py:61
  79.3 0.2 reshape.194
  79.5 0.4 convolution_convert_fusion.3
  79.9 0.4 convolution_convert_fusion.4
  80.3 0.1 copy-done.6
  80.4 0.4 convolution_convert_fusion.5
  80.8 0.3 convolution_multiply_fusion
  81.2 0.3 convolution_multiply_fusion.1
  81.5 31.0 %select_reduce_fusion.2 = (f32[512]{0:T(512)S(1)}, f32[512]{0:T(512)S(1)}, f32[512]{0:T(512)S(1)}, f32[512,512]{0,1:T(8,128)S(1)}) fusion(pred[]{:T(512)S(6)} %lt.77, s32[]{:T(128)S(6)} %select_n.89, pred[512]{0:T(512)(128)(4,1)S(1)} %fusion.34, s32[512]{0:T(512)S(1)} %convert_reduce_fusion, f32[512,512]{0,1:T(8,128)S(1)} %convolution_multiply_fusion.1, ...), kind=kOutput, calls=%fused_computation.33 | convolution fusion | flops 43776512 | bytes 3287567 | tf_op jit(solution)/shard_map/dot_general | solution.py:92
  112.5 31.6 %fusion.25 = (f32[512]{0:T(512)S(1)}, f32[512]{0:T(512)S(1)}, f32[512]{0:T(512)S(1)}) fusion(f32[512,512]{0,1:T(8,128)S(1)} %get-tuple-element.55, f32[512]{0:T(512)S(1)} %get-tuple-element.42, pred[]{:T(512)S(6)} %lt.77, s32[]{:T(128)S(6)} %select_n.89, pred[512]{0:T(512)(128)(4,1)S(1)} %fusion.34, s32[512]{0:T(512)S(1)} %convert_reduce_fusion, ...), kind=kLoop, calls=%fused_computation.56 | loop fusion | flops 10746368 | bytes 3160591 | tf_op jit(solution)/shard_map/reduce_sum | solution.py:99
  144.2 10.6 %convolution_convert_fusion.6 = bf16[512,64]{0,1:T(8,128)(2,1)S(1)} fusion(f32[512,512]{0,1:T(8,128)S(1)} %convolution_multiply_fusion, f32[512]{0:T(512)S(1)} %get-tuple-element.41, f32[512]{0:T(512)S(1)} %get-tuple-element.44, pred[]{:T(512)S(6)} %lt.83, s32[]{:T(128)S(6)} %select_n.99, pred[512]{0:T(512)(128)(4,1)S(1)} %fusion.34, ...), kind=kOutput, calls=%fused_computation.14 | convolution fusion | flops 38305792 | bytes 1188357 | tf_op jit(solution)/shard_map/dot_general | solution.py:101
  154.7 10.7 %convolution_convert_fusion.7 = bf16[512,64]{0,1:T(8,128)(2,1)S(1)} fusion(f32[512,512]{0,1:T(8,128)S(1)} %convolution_multiply_fusion.1, f32[512]{0:T(512)S(1)} %get-tuple-element.40, f32[512]{0:T(512)S(1)} %get-tuple-element.43, pred[]{:T(512)S(6)} %lt.80, s32[]{:T(128)S(6)} %select_n.94, pred[512]{0:T(512)(128)(4,1)S(1)} %fusion.34, ...), kind=kOutput, calls=%fused_computation.15 | convolution fusion | flops 38305792 | bytes 1188357 | tf_op jit(solution)/shard_map/dot_general | solution.py:101
  165.5 10.8 %convolution_convert_fusion.8 = bf16[512,64]{0,1:T(8,128)(2,1)S(1)} fusion(f32[512,512]{0,1:T(8,128)S(1)} %get-tuple-element.55, f32[512]{0:T(512)S(1)} %get-tuple-element.39, f32[512]{0:T(512)S(1)} %get-tuple-element.42, pred[]{:T(512)S(6)} %lt.77, s32[]{:T(128)S(6)} %select_n.89, pred[512]{0:T(512)(128)(4,1)S(1)} %fusion.34, ...), kind=kOutput, calls=%fused_computation.16 | convolution fusion | flops 38305792 | bytes 1188357 | tf_op jit(solution)/shard_map/dot_general | solution.py:101
  176.3 0.5 broadcast.147
  176.8 0.7 reduce.9
  177.6 0.1 copy.83
  177.7 1.0 reshape.235
  178.7 9.6 %all-to-all-start.1 = ((bf16[128,2,384]{2,1,0:T(2,128)(2,1)}), bf16[128,2,384]{2,1,0:T(2,128)(2,1)S(1)}, u32[]{:S(2)}, u32[]{:S(2)}) async-start(bf16[128,2,384]{2,1,0:T(2,128)(2,1)} %reshape.235), calls=%async_computation.1 | async-start | bytes 393216 | tf_op jit(solution)/shard_map/all_to_all | solution.py:104
  188.4 0.3 reduce-scatter.7.cloned.1.call-start
  188.7 0.1 reshape.201
  188.9 0.1 copy.65
  189.0 0.2 fusion.28
  189.3 0.1 fusion.48
  189.4 0.1 convert_element_type.99
  189.5 0.2 convolution_convert_fusion.9
  189.7 0.8 copy.69
  190.6 15.8 %all-to-all-done.1 = bf16[128,2,384]{2,1,0:T(2,128)(2,1)S(1)} async-done(((bf16[128,2,384]{2,1,0:T(2,128)(2,1)}), bf16[128,2,384]{2,1,0:T(2,128)(2,1)S(1)}, u32[]{:S(2)}, u32[]{:S(2)}) %all-to-all-start.1) | async-done | bytes 196640 | tf_op jit(solution)/shard_map/all_to_all | solution.py:104
  206.3 0.3 reshape.236
  206.7 1.7 reduce.6
  208.4 0.2 copy.50
  208.7 1.3 convolution_convert_fusion
  210.0 0.2 fusion.60
  210.2 0.1 mul.91
  210.4 0.2 copy.55
  210.6 0.6 broadcast_multiply_fusion
  211.2 0.6 reshape.216
  211.7 3.5 %scatter_custom_fusion = f32[768,192]{1,0:T(8,128)S(1)} fusion(s32[512]{0:T(512)S(1)} %bitcast.74, f32[512,192]{1,0:T(8,128)S(1)} %reshape.216, f32[]{:T(128)} %constant.136.clone.1), kind=kCustom, calls=%fused_computation.65 | custom fusion | flops 98304 | bytes 589828 | tf_op jit(solution)/shard_map/scatter-add | solution.py:163
  215.3 4.3 %collective-permute-start.2 = (bf16[128,192]{1,0:T(8,128)(2,1)S(1)}, bf16[128,192]{1,0:T(8,128)(2,1)S(1)}, u32[]{:S(2)}, u32[]{:S(2)}) collective-permute-start(bf16[128,192]{1,0:T(8,128)(2,1)S(1)} %get-tuple-element.48), channel_id=1, source_target_pairs={{0,4},{4,8},{8,12},{12,16},{16,20},{20,24},{24,28},{28,32},{32,36}... | collective-permute-start | bytes 147464 | tf_op jit(solution)/shard_map/ppermute | solution.py:29
  219.7 1.9 collective-permute-start.3
  221.7 3.6 %collective-permute-done.3 = bf16[128,192]{1,0:T(8,128)(2,1)S(1)} collective-permute-done((bf16[128,192]{1,0:T(8,128)(2,1)S(1)}, bf16[128,192]{1,0:T(8,128)(2,1)S(1)}, u32[]{:S(2)}, u32[]{:S(2)}) %collective-permute-start.3) | collective-permute-done | bytes 49184 | tf_op jit(solution)/shard_map/ppermute | solution.py:29
  225.4 0.8 copy.56
  226.2 1.5 copy.70
  227.6 25.9 %reduce-scatter.5.cloned.1.call-done = bf16[512,192]{0,1:T(8,128)(2,1)} async-done(((bf16[512,768]{0,1:T(8,128)(2,1)}), bf16[512,192]{0,1:T(8,128)(2,1)}) %reduce-scatter.5.cloned.1.call-update) | async-done | bytes 196624 | tf_op jit(solution)/shard_map/reduce_scatter | solution.py:113
  (63 shorter events, 1.3 us)
Async XLA Ops:
  7.2 201.5 %copy-start = (bf16[192,768]{1,0:T(8,128)(2,1)S(1)}, bf16[192,768]{1,0:T(8,128)(2,1)}, u32[]{:S(2)}) copy-start(bf16[192,768]{1,0:T(8,128)(2,1)} %param.27) | copy-start | bytes 884740
  7.2 1.7 copy-start.1
  7.2 1.7 copy-start.3
  9.4 30.7 %collective-permute-start = (bf16[128,384]{0,1:T(8,128)(2,1)S(1)}, bf16[128,384]{0,1:T(8,128)(2,1)S(1)}, u32[]{:S(2)}, u32[]{:S(2)}) collective-permute-start(bf16[128,384]{0,1:T(8,128)(2,1)S(1)} %get-tuple-element.51), channel_id=1, source_target_pairs={{0,4},{4,8},{8,12},{12,16},{16,20},{20,24},{24,28},{28,32},{32,36}... | collective-permute-start | bytes 294920 | tf_op jit(solution)/shard_map/ppermute | solution.py:17
  14.0 26.1 %collective-permute-start.1 = (bf16[128,384]{0,1:T(8,128)(2,1)S(1)}, bf16[128,384]{0,1:T(8,128)(2,1)S(1)}, u32[]{:S(2)}, u32[]{:S(2)}) collective-permute-start(bf16[128,384]{0,1:T(8,128)(2,1)S(1)} %get-tuple-element.52), channel_id=1, source_target_pairs={{4,0},{8,4},{12,8},{16,12},{20,16},{24,20},{28,24},{32,28},{36,32}... | collective-permute-start | bytes 294920 | tf_op jit(solution)/shard_map/ppermute | solution.py:19
  21.0 17.0 %copy-start.5 = (bf16[32,768]{1,0:T(8,128)(2,1)S(1)}, bf16[32,768]{1,0:T(8,128)(2,1)}, u32[]{:S(2)}) copy-start(bf16[32,768]{1,0:T(8,128)(2,1)} %param.20) | copy-start | bytes 147460
  21.0 17.2 %copy-start.7 = (bf16[768,192]{0,1:T(8,128)(2,1)S(1)}, bf16[768,192]{0,1:T(8,128)(2,1)}, u32[]{:S(2)}) copy-start(bf16[768,192]{0,1:T(8,128)(2,1)} %param.28) | copy-start | bytes 884740
  21.0 17.7 %copy-start.12 = (s32[8]{0:T(128)S(1)}, s32[8]{0:T(128)}, u32[]{:S(2)}) copy-start(s32[8]{0:T(128)} %param.19) | copy-start | bytes 100
  21.0 17.9 %copy-start.10 = (s32[32,16]{0,1:T(8,128)S(1)}, s32[32,16]{0,1:T(8,128)}, u32[]{:S(2)}) copy-start(s32[32,16]{0,1:T(8,128)} %param.21) | copy-start | bytes 6148
  21.0 18.4 %copy-start.2 = (bf16[768,192]{0,1:T(8,128)(2,1)S(1)}, bf16[768,192]{0,1:T(8,128)(2,1)}, u32[]{:S(2)}) copy-start(bf16[768,192]{0,1:T(8,128)(2,1)} %param.26) | copy-start | bytes 884740
  21.0 58.3 %all-to-all-start = ((bf16[4,128,768]{2,0,1:T(4,128)(2,1)}), bf16[4,128,768]{2,0,1:T(4,128)(2,1)S(1)}, u32[]{:S(2)}, u32[]{:S(2)}) async-start(bf16[4,128,768]{2,0,1:T(4,128)(2,1)} %copy.48), calls=%async_computation | async-start | bytes 1572864 | tf_op jit(solution)/shard_map/all_to_all | solution.py:61
  37.9 1.8 copy-start.11
  37.9 1.9 copy-start.8
  79.5 1.0 copy-start.6
  178.7 10.8 %copy-start.4 = (bf16[192,768]{1,0:T(8,128)(2,1)S(1)}, bf16[192,768]{1,0:T(8,128)(2,1)}, u32[]{:S(2)}) copy-start(bf16[192,768]{1,0:T(8,128)(2,1)} %param.29) | copy-start | bytes 884740
  178.7 27.6 %all-to-all-start.1 = ((bf16[128,2,384]{2,1,0:T(2,128)(2,1)}), bf16[128,2,384]{2,1,0:T(2,128)(2,1)S(1)}, u32[]{:S(2)}, u32[]{:S(2)}) async-start(bf16[128,2,384]{2,1,0:T(2,128)(2,1)} %reshape.235), calls=%async_computation.1 | async-start | bytes 393216 | tf_op jit(solution)/shard_map/all_to_all | solution.py:104
  188.4 37.8 %reduce-scatter.7.cloned.1.call-start = ((), (), s32[]{:S(2)}) async-start(), calls=%async_computation.5 | async-start | bytes 245760
  190.5 63.0 %reduce-scatter.5.cloned.1.call-start = ((), (), s32[]{:S(2)}) async-start(), calls=%async_computation.4 | async-start | bytes 983040 | tf_op jit(solution)/shard_map/reduce_scatter | solution.py:113
  208.7 1.3 copy-start.9
  215.3 6.3 %collective-permute-start.2 = (bf16[128,192]{1,0:T(8,128)(2,1)S(1)}, bf16[128,192]{1,0:T(8,128)(2,1)S(1)}, u32[]{:S(2)}, u32[]{:S(2)}) collective-permute-start(bf16[128,192]{1,0:T(8,128)(2,1)S(1)} %get-tuple-element.48), channel_id=1, source_target_pairs={{0,4},{4,8},{8,12},{12,16},{16,20},{20,24},{24,28},{28,32},{32,36}... | collective-permute-start | bytes 147464 | tf_op jit(solution)/shard_map/ppermute | solution.py:29
  219.7 5.6 %collective-permute-start.3 = (bf16[128,192]{1,0:T(8,128)(2,1)S(1)}, bf16[128,192]{1,0:T(8,128)(2,1)S(1)}, u32[]{:S(2)}, u32[]{:S(2)}) collective-permute-start(bf16[128,192]{1,0:T(8,128)(2,1)S(1)} %get-tuple-element.47), channel_id=1, source_target_pairs={{4,0},{8,4},{12,8},{16,12},{20,16},{24,20},{28,24},{32,28},{36,32}... | collective-permute-start | bytes 147464 | tf_op jit(solution)/shard_map/ppermute | solution.py:29
Sparse Core Ops, SparseCore 0:
  192.0 26.7 reduce-scatter.6
  222.5 31.0 reduce-scatter.4
where the time goes:
time: 266 us; the launch traced here: 261 us
  waiting for transfers between devices  80.9 us (30%)
  matrix products  69.9 us (26%)
  starting transfers between devices  43.2 us (16%)
  other arithmetic  39.4 us (15%)
  between operations  15.2 us (6%)
  local copies, waits for them, and re-layouts  12.3 us (5%)
    all_to_all x1, waiting for transfers between devices, body(): lax.all_to_all(tile_rows.reshape(stride_rows, groups, model_width), 'seq'...  35.6 us
    dot_general x3, matrix products, body(): jnp.dot(weights, value_head, preferred_element_type=jnp.float32)  32.1 us
    dot_general x3, matrix products, body(): lax.dot_general(query_head, key_head, (((1,), (1,)), ((), ())), preferred...  31.7 us
    reduce_sum x1, other arithmetic, body(): jnp.sum(expon, axis=1, keepdims=True)  31.6 us
    reduce_scatter x1, waiting for transfers between devices, body(): lax.psum_scatter(partial_sums.astype(jnp.bfloat16), 'head', scatter_dimen...  25.9 us
    all_to_all x1, starting transfers between devices, body(): lax.all_to_all(tile_rows.reshape(stride_rows, groups, model_width), 'seq'...  16.9 us
    all_to_all x1, waiting for transfers between devices, body(): lax.all_to_all(attended_class.reshape(rows_dev, 1, head_cols), 'seq', spl...  15.8 us
    all_to_all x1, starting transfers between devices, body(): lax.all_to_all(attended_class.reshape(rows_dev, 1, head_cols), 'seq', spl...  9.63 us
  transfers between devices with their start and end apart: 8, of which 4 were waited for; matrix products, arithmetic and copies ran while one was open for 8% of the time, Pallas kernels for 0%

commit v1 on v0

v1 whole, which is shorter than its diff:
```python
import functools

import jax
import jax.numpy as jnp
from jax import lax
from jax.experimental import pallas as pl
from jax.experimental.pallas import tpu as pltpu
from jax.sharding import PartitionSpec as P

HD = 64
NZ = 16
NQ = 8
NX = 4
MESH = pl.DeviceIdType.MESH
F32 = jnp.float32
BF16 = jnp.bfloat16
NEG = -1e30
ZORDER = (1, 15, 2, 14, 3, 13, 4, 12, 5, 11, 6, 10, 7, 9, 8)


def iota(shape, dim):
    return lax.broadcasted_iota(jnp.int32, shape, dim)


def nt(a, b):
    return lax.dot_general(a, b, (((1,), (1,)), ((), ())), preferred_element_type=F32)


def tn(a, b):
    return lax.dot_general(a, b, (((0,), (0,)), ((), ())), preferred_element_type=F32)


def mm(a, b):
    return jnp.dot(a, b, preferred_element_type=F32)


def order_of(row):
    return (row & ~31) | ((row & 7) << 2) | ((row >> 3) & 3)


def kernel(
    lengths,
    tiles,
    tissue,
    regions,
    parents,
    counts,
    cotangent,
    w_all,
    w_cq,
    wo4,
    wco4,
    wco,
    out_tile,
    out_region,
    out_grad,
    first,
    second,
    feats,
    qkv,
    ext,
    wrecv,
    wlast,
    att,
    zout,
    zin,
    pout,
    pin,
    gext,
    gown,
    gprev,
    gnext,
    rout,
    rin,
    perm_a,
    perm_b,
    p1s,
    p1r,
    p2s,
    p2r,
    pxs,
    pxr,
    wos,
    wor,
    has,
    har,
    axs,
    axr,
    zas,
    zar,
    pbs,
    pbr,
    grs,
    grr,
    res,
    rer,
):
    s = lax.axis_index("seq")
    x = lax.axis_index("head")
    z = s // NQ
    q = lax.rem(s, NQ)
    n_seq = NZ * NQ
    after = lax.rem(s + 1, n_seq)
    before = lax.rem(s + n_seq - 1, n_seq)

    def remote(src, dst, ss, rs, seq, head):
        return pltpu.make_async_remote_copy(
            src_ref=src,
            dst_ref=dst,
            send_sem=ss,
            recv_sem=rs,
            device_id={"seq": seq, "head": head},
            device_id_type=MESH,
        )

    sent = []

    def go(*args):
        copy = remote(*args)
        copy.start()
        sent.append(copy)
        return copy

    barrier = pltpu.get_barrier_semaphore()

    def greet(seq, head):
        pl.semaphore_signal(
            barrier, inc=1, device_id={"seq": seq, "head": head}, device_id_type=MESH
        )

    for d in range(1, NQ):
        greet(z * NQ + lax.rem(q + d, NQ), x)
    for d in ZORDER:
        greet(lax.rem(z + d, NZ) * NQ + q, x)
    for d in range(1, NX):
        greet(s, lax.rem(x + d, NX))
    greet(after, x)
    greet(before, x)
    pl.semaphore_wait(barrier, (NQ - 1) + (NZ - 1) + (NX - 1) + 2)

    hop1 = []
    for d in range(1, NQ):
        to = lax.rem(q + d, NQ)
        hop1.append(
            go(
                tiles.at[pl.ds(pl.multiple_of(x * 128 + to * 16, 16), 16)],
                first.at[pl.ds(pl.multiple_of(q * 16, 16), 16)],
                p1s.at[d],
                p1r.at[d],
                z * NQ + to,
                x,
            )
        )
    first[pl.ds(pl.multiple_of(q * 16, 16), 16), :] = tiles[
        pl.ds(pl.multiple_of(x * 128 + q * 16, 16), 16), :
    ]
    wcopies = []
    for d in range(1, NX):
        to = lax.rem(x + d, NX)
        wcopies.append(go(wo4.at[to], wrecv.at[x], wos.at[d], wor.at[d], s, to))
    wrecv[x] = wo4[x]

    block = tiles[...]
    ext[128:640, 0:256] = mm(block, w_all[:, 128:384]).astype(BF16)
    ext[128:640, 256:384] = mm(block, w_all[:, 512:640]).astype(BF16)
    halos = [
        go(ext.at[128:256], ext.at[640:768], has.at[0], har.at[0], before, x),
        go(ext.at[512:640], ext.at[0:128], has.at[1], har.at[1], after, x),
    ]

    lane = iota((256, 128), 1)
    row = iota((256, 128), 0)
    source = (lane & 15) * 16 + (lane >> 4)
    left = (source == row).astype(BF16)
    right = (source + 8 == row).astype(BF16)
    for copy in hop1:
        copy.wait_recv()
    second[...] = (
        (mm(left, first[:, 0:384]) + mm(right, first[:, 384:768]))
        .astype(BF16)
        .reshape(NZ, 16, 384)
    )
    hop2 = {}
    for d in ZORDER:
        to = lax.rem(z + d, NZ)
        hop2[d] = go(second.at[to], feats.at[z, x], p2s.at[d], p2r.at[d], to * NQ + q, x)
    feats[z, x] = second[z]

    hopx = []

    def spread(d):
        at = lax.rem(z - d + NZ, NZ)
        for e in range(1, NX):
            to = lax.rem(x + e, NX)
            hopx.append(
                go(feats.at[at, x], feats.at[at, x], pxs.at[e, d], pxr.at[e, d], s, to)
            )

    spread(0)
    for d in ZORDER:
        hop2[d].wait_recv()
        spread(d)

    low = iota((32, 128), 1) < HD
    rows32 = regions[...]
    cq = (mm(rows32, w_cq[...]).astype(BF16)).astype(F32) * (HD**-0.5)
    rk = mm(rows32, w_all[:, 128:384]).astype(BF16).astype(F32)
    rkv2 = mm(rows32, w_all[:, 512:640]).astype(BF16).astype(F32)
    rk01, rv01 = rk[:, 0:128], rk[:, 128:256]
    cq0 = jnp.where(low, cq[:, 0:128], 0.0)
    cq1 = jnp.where(low, 0.0, cq[:, 0:128])
    cq2 = jnp.where(low, cq[:, 128:256], 0.0)
    back = nt(cotangent[...], wco[...]).astype(BF16)
    place = iota((32, 768), 1)
    times = jnp.zeros((32, 768), F32)
    base = s * 512 - 128
    count = counts[...]
    lists = parents[...] - base
    for j in range(16):
        hit = (lists[:, j : j + 1] == place) & (j < count)
        times = times + jnp.where(hit, 1.0, 0.0)
    valid = times > 0.0
    for copy in halos:
        copy.wait_recv()
    outs = []
    grads = []
    for h in range(3):
        query = (cq0, cq1, cq2)[h]
        own = jnp.sum(query * (rk01 if h < 2 else rkv2), axis=1, keepdims=True)
        keys = ext[:, 0:128] if h < 2 else ext[:, 256:384]
        values = ext[:, 128:256] if h < 2 else keys
        sc = jnp.where(valid, nt(query.astype(BF16), keys), NEG)
        top = jnp.maximum(own, jnp.max(sc, axis=1, keepdims=True))
        ex = jnp.where(valid, jnp.exp(sc - top), 0.0)
        ex_own = jnp.exp(own - top)
        total = ex_own + jnp.sum(times * ex, axis=1, keepdims=True)
        weight = (ex / total).astype(BF16).astype(F32)
        weight_own = (ex_own / total).astype(BF16).astype(F32)
        mixed = (times * weight).astype(BF16)
        outs.append(mm(mixed, values) + weight_own * (rv01 if h < 2 else rkv2))
        grads.append(tn(mixed, back[:, 0:128] if h < 2 else back[:, 128:192]))
    cross_a = jnp.where(low, outs[0], outs[1]).astype(BF16)
    cross_b = pltpu.roll(outs[2], 64, 1)[:, 0:64].astype(BF16)
    low768 = iota((768, 128), 1) < HD
    grad_a = jnp.where(low768, grads[0], grads[1])
    grad_b = grads[2]
    gown[:, 0:128] = grad_a[128:640]
    gown[:, 128:192] = grad_b[128:640]
    zero = jnp.zeros((128, 64), BF16)
    gext[0:128, 0:128] = grad_a[0:128].astype(BF16)
    gext[0:128, 128:256] = jnp.concatenate([grad_b[0:128].astype(BF16), zero], axis=1)
    gext[128:256, 0:128] = grad_a[640:768].astype(BF16)
    gext[128:256, 128:256] = jnp.concatenate([grad_b[640:768].astype(BF16), zero], axis=1)
    gcopies = [
        go(gext.at[0:128], gnext, grs.at[0], grr.at[0], before, x),
        go(gext.at[128:256], gprev, grs.at[1], grr.at[1], after, x),
    ]
    for g in range(NX):
        rout[g] = (mm(cross_a, wco4[g, 0:128]) + mm(cross_b, wco4[g, 128:192])).astype(BF16)
    rcopies = []
    for d in range(1, NX):
        to = lax.rem(x + d, NX)
        rcopies.append(go(rout.at[to], rin.at[x], res.at[d], rer.at[d], s, to))
    rin[x] = rout[x]

    prow = iota((512, 512), 0)
    pcol = iota((512, 512), 1)
    perm_a[...] = (
        ((prow & 15) * 32 + ((prow >> 4) & 3) * 8 + (prow >> 6)) == pcol
    ).astype(BF16)
    prow = iota((256, 256), 0)
    pcol = iota((256, 256), 1)
    perm_b[...] = (
        ((prow & 15) * 16 + ((prow >> 4) & 1) * 8 + (prow >> 5)) == pcol
    ).astype(BF16)
    wlast[:, 0:64] = jnp.zeros((NX, 64, 256), BF16)
    wlast[:, 128:192] = jnp.zeros((NX, 64, 256), BF16)

    c = q * NZ + z
    pick = (iota((16, 128), 1) == c).astype(BF16)
    tissue_n = nt(pick, tissue[...].astype(F32).astype(BF16)).astype(BF16)
    spread_n = (iota((512, 512), 0) == order_of(iota((512, 512), 1))).astype(BF16)
    tissue_row = mm(tissue_n, spread_n)[0:1]
    n_row = order_of(iota((1, 512), 1))
    slide_row = jnp.zeros((1, 512), jnp.int32)
    end = jnp.int32(0)
    for k in range(8):
        end = end + lengths[k]
        slide_row = slide_row + jnp.where(n_row * 128 + c >= end, 1, 0)

    for copy in hopx:
        copy.wait_recv()

    for b in range(4):
        part = feats[4 * b : 4 * b + 4].astype(F32).reshape(16, 2, 8, 384)
        left = part[:, 0].reshape(128, 384).astype(BF16)
        right = part[:, 1].reshape(128, 384).astype(BF16)
        qkv[128 * b : 128 * b + 128] = (
            mm(left, w_all[0:384]) + mm(right, w_all[384:768])
        ).astype(BF16)

    low128 = iota((128, 128), 1) < HD
    keys01 = qkv[:, 128:256].astype(F32)
    low512 = iota((512, 128), 1) < HD
    key0 = jnp.where(low512, keys01, 0.0).astype(BF16)
    key1 = jnp.where(low512, 0.0, keys01).astype(BF16)
    key_value2 = qkv[:, 512:640]
    values01 = qkv[:, 256:384]
    has_tissue = tissue_row > 0.5
    own_chunk = z // 4
    low64 = iota((64, 128), 1) < HD

    acopies = {}
    for j in range(4):
        chunk = lax.rem(own_chunk + j, 4)
        at = pl.multiple_of(chunk * 128, 128)
        query01 = (qkv[pl.ds(at, 128), 0:128].astype(F32) * (HD**-0.5)).astype(BF16)
        query2 = (qkv[pl.ds(at, 128), 384:512].astype(F32) * (HD**-0.5)).astype(BF16)
        row = iota((128, 1), 0) + at
        n_mine = order_of(row)
        slide_mine = jnp.zeros((128, 1), jnp.int32)
        end = jnp.int32(0)
        for k in range(8):
            end = end + lengths[k]
            slide_mine = slide_mine + jnp.where(n_mine * 128 + c >= end, 1, 0)
        base_ok = (slide_mine == slide_row) & (has_tissue | (row == iota((128, 512), 1)))
        parts = []
        for h in range(3):
            step = (jnp.int32(1) << lax.rem(3 * x + h, 4)) - 1
            allowed = base_ok & ((n_mine & step) == (n_row & step))
            sc = nt(query01 if h < 2 else query2, (key0, key1, key_value2)[h])
            sc = jnp.where(allowed, sc, NEG)
            ex = jnp.exp(sc - jnp.max(sc, axis=1, keepdims=True))
            total = jnp.sum(ex, axis=1, keepdims=True)
            parts.append(mm(ex.astype(BF16), values01 if h < 2 else key_value2) / total)
        att[x, chunk, 0:128] = jnp.where(low128, parts[0], parts[1]).astype(BF16)
        att[x, chunk, 128:192] = jnp.where(
            low64, pltpu.roll(parts[2][0:64], 64, 1), parts[2][64:128]
        ).astype(BF16)
        for e in range(1, NX):
            to = lax.rem(x + e, NX)
            acopies[e, j] = go(
                att.at[x, chunk], att.at[x, chunk], axs.at[e, j], axr.at[e, j], s, to
            )
        if j == 0:
            for copy in wcopies:
                copy.wait_recv()
            wlast[:, 64:128] = wrecv[:, 128:192]
        if j > 0:
            finish(acopies, j - 1, own_chunk, att, wrecv, wlast, zout, low64)
            send_z(go, zout, zin, zas, zar, own_chunk, j - 1, z, q, x)
    finish(acopies, 3, own_chunk, att, wrecv, wlast, zout, low64)
    send_z(go, zout, zin, zas, zar, own_chunk, 3, z, q, x)
    zin[z] = zout[z]

    for copy in gcopies + rcopies:
        copy.wait_recv()
    gown[0:128, 0:192] = gown[0:128, 0:192] + gprev[:, 0:192].astype(F32)
    gown[384:512, 0:192] = gown[384:512, 0:192] + gnext[:, 0:192].astype(F32)
    out_grad[...] = gown[:, 0:192].astype(BF16)
    total = rin[0].astype(F32)
    for g in range(1, NX):
        total = total + rin[g].astype(F32)
    out_region[...] = total[:, 0:192].astype(BF16)

    for d in range(1, NZ):
        copy = remote(
            zout.at[z], zin.at[z], zas.at[d], zar.at[d], lax.rem(z + d, NZ) * NQ + q, x
        )
        copy.wait_recv()
        sent.append(copy)
    rows_a = mm(perm_a[...], zin[:, 0:32].reshape(512, 128)).astype(BF16)
    rows_b = mm(perm_b[...], zin[:, 32:48].reshape(256, 128)).astype(BF16)
    pout[:, 0:64] = rows_a.reshape(NQ, 64, 128)
    pout[:, 64:96] = rows_b.reshape(NQ, 32, 128)
    backs = []
    for d in range(1, NQ):
        to = lax.rem(q + d, NQ)
        backs.append(go(pout.at[to], pin.at[q], pbs.at[d], pbr.at[d], z * NQ + to, x))
    pin[q] = pout[q]
    for copy in backs:
        copy.wait_recv()
    for p in range(NQ):
        half = pin[p, 64:96].astype(F32)
        turned = pltpu.roll(half, 64, 1)
        for i in range(4):
            at = i * 128 + p * 16
            out_tile[at : at + 16, 0:128] = pin[p, 16 * i : 16 * i + 16]
            k = (i & 1) * 16
            out_tile[at : at + 16, 128:192] = (half if i < 2 else turned)[
                k : k + 16, 0:64
            ].astype(BF16)
    for copy in sent:
        copy.wait_send()


def finish(acopies, j, own_chunk, att, wrecv, wlast, zout, low64):
    for e in range(1, NX):
        acopies[e, j].wait_recv()
    chunk = lax.rem(own_chunk + j, 4)
    acc = jnp.zeros((128, 256), F32)
    upper = jnp.zeros((64, 256), F32)
    lower = jnp.zeros((64, 256), F32)
    for g in range(NX):
        acc = acc + mm(att[g, chunk, 0:128], wrecv[g, 0:128])
        upper = upper + mm(att[g, chunk, 128:192], wlast[g, 64:192])
        lower = lower + mm(att[g, chunk, 128:192], wlast[g, 0:128])
    acc = acc + jnp.concatenate([upper, lower], axis=0)
    two = acc[:, 128:256].reshape(4, 2, 16, 128)
    packed = jnp.where(
        low64,
        two[:, 0].reshape(64, 128),
        pltpu.roll(two[:, 1].reshape(64, 128), 64, 1),
    )
    at = chunk * 4
    zout[pl.ds(at, 4), 0:32] = acc[:, 0:128].reshape(4, 32, 128).astype(BF16)
    zout[pl.ds(at, 4), 32:48] = packed.reshape(4, 16, 128).astype(BF16)


def send_z(go, zout, zin, zas, zar, own_chunk, j, z, q, x):
    for k in range(4):
        to = lax.rem(own_chunk + j, 4) * 4 + k
        d = lax.rem(to - z + NZ, NZ)

        @pl.when(d != 0)
        def _():
            copy = pltpu.make_async_remote_copy(
                src_ref=zout.at[to],
                dst_ref=zin.at[z],
                send_sem=zas.at[d],
                recv_sem=zar.at[d],
                device_id={"seq": to * NQ + q, "head": x},
                device_id_type=MESH,
            )
            copy.start()


def body(
    tile_rows,
    tissue_mask,
    slide_lengths,
    region_rows,
    parent_lists,
    child_counts,
    region_cotangent,
    w_query,
    w_key,
    w_value,
    w_output,
    w_cross_query,
    w_cross_output,
):
    pad = ((0, 0), (0, 64))
    w_all = jnp.concatenate(
        [
            w_query[:, :128],
            w_key[:, :128],
            w_value[:, :128],
            jnp.pad(w_query[:, 128:], pad),
            w_key[:, 128:],
            w_value[:, 128:],
        ],
        axis=1,
    )
    w_cq = jnp.pad(w_cross_query, pad)
    split = lambda w: jnp.transpose(
        jnp.pad(w.reshape(192, NX, 192), ((0, 0), (0, 0), (0, 64))), (1, 0, 2)
    )
    dma = pltpu.SemaphoreType.DMA
    vmem = lambda *shape: pltpu.VMEM(shape, BF16)
    return pl.pallas_call(
        kernel,
        out_shape=(
            jax.ShapeDtypeStruct((512, 192), BF16),
            jax.ShapeDtypeStruct((32, 192), BF16),
            jax.ShapeDtypeStruct((512, 192), BF16),
        ),
        in_specs=[pl.BlockSpec(memory_space=pltpu.SMEM)]
        + [pl.BlockSpec(memory_space=pltpu.VMEM)] * 11,
        out_specs=(pl.BlockSpec(memory_space=pltpu.VMEM),) * 3,
        scratch_shapes=[
            vmem(128, 768),
            vmem(16, 16, 384),
            vmem(16, 4, 16, 384),
            vmem(512, 640),
            vmem(768, 384),
            vmem(4, 192, 256),
            vmem(4, 192, 256),
            vmem(4, 4, 192, 128),
            vmem(16, 48, 128),
            vmem(16, 48, 128),
            vmem(8, 96, 128),
            vmem(8, 96, 128),
            vmem(256, 256),
            pltpu.VMEM((512, 256), F32),
            vmem(128, 256),
            vmem(128, 256),
            vmem(4, 32, 256),
            vmem(4, 32, 256),
            vmem(512, 512),
            vmem(256, 256),
            dma((8,)),
            dma((8,)),
            dma((16,)),
            dma((16,)),
            dma((4, 16)),
            dma((4, 16)),
            dma((4,)),
            dma((4,)),
            dma((2,)),
            dma((2,)),
            dma((4, 4)),
            dma((4, 4)),
            dma((16,)),
            dma((16,)),
            dma((8,)),
            dma((8,)),
            dma((2,)),
            dma((2,)),
            dma((4,)),
            dma((4,)),
        ],
        compiler_params=pltpu.CompilerParams(
            collective_id=0, has_side_effects=True, vmem_limit_bytes=48 * 1024 * 1024
        ),
    )(
        slide_lengths,
        tile_rows,
        tissue_mask.reshape(512, 128),
        region_rows,
        parent_lists,
        child_counts.reshape(32, 1),
        region_cotangent,
        w_all,
        w_cq,
        split(w_output),
        split(w_cross_output),
        w_cross_output,
    )


def solution(mesh):
    in_specs = (
        P("seq", None),
        P(),
        P(),
        P("seq", None),
        P("seq", None),
        P("seq"),
        P("seq", None),
        P(None, "head"),
        P(None, "head"),
        P(None, "head"),
        P("head", None),
        P(None, "head"),
        P("head", None),
    )
    out_specs = (P("seq", "head"), P("seq", "head"), P("seq", "head"))
    return jax.shard_map(body, mesh=mesh, in_specs=in_specs, out_specs=out_specs, check_vma=False)
```

time: 266 us -> 90.4 us (0.34); the launches traced: 261 us -> 89.8 us
  waiting for transfers between devices: 80.9 us -> 0 us
  matrix products: 69.9 us -> 0 us
  Pallas kernels: 0 us -> 68.9 us
  starting transfers between devices: 43.2 us -> 0 us
  other arithmetic: 39.4 us -> 0 us
  between operations: 15.2 us -> 0.8 us
  local copies, waits for them, and re-layouts: 12.3 us -> 20.1 us
    dot_general x19 -> x0, matrix products: 69.9 us -> none  [the longest x3 32.1 us: body(): jnp.dot(weights, value_head, preferred_element_type=jnp.float32)]
    pallas_call x0 -> x1, Pallas kernels: none -> 68.9 us  [body(): pl.pallas_call(kernel, out_shape=(jax.ShapeDtypeStruct((512, 192), BF16),...]
    all_to_all x2 -> x0, waiting for transfers between devices: 51.4 us -> none  [the longest x1 35.6 us: body(): lax.all_to_all(tile_rows.reshape(stride_rows, groups, model_width), 'seq'...]
    reduce_sum x3 -> x0, other arithmetic: 31.7 us -> none  [the longest x1 31.6 us: body(): jnp.sum(expon, axis=1, keepdims=True)]
    all_to_all x2 -> x0, starting transfers between devices: 26.5 us -> none  [the longest x1 16.9 us: body(): lax.all_to_all(tile_rows.reshape(stride_rows, groups, model_width), 'seq'...]
    reduce_scatter x1 -> x0, waiting for transfers between devices: 25.9 us -> none  [body(): lax.psum_scatter(partial_sums.astype(jnp.bfloat16), 'head', scatter_dimen...]
    ppermute x4 -> x0, starting transfers between devices: 16.3 us -> none  [the longest x2 6.27 us: shifted(): return lax.ppermute(array, axis, pairs)]
    slice x4 -> x12, local copies, waits for them, and re-layouts: 0.29 us -> 5.45 us  [the longest x2 0.93 us: body(): w_key[:, :128]]
  transfers between devices with their start and end apart: 8 -> 0, of which waited for: 4 -> 0; matrix products, arithmetic and copies ran while one was open for 8% -> 0% of each run, Pallas kernels for 0% -> 0%
where the time goes in v1:
time: 90.4 us; the launch traced here: 89.8 us
  Pallas kernels  68.9 us (76%)
  local copies, waits for them, and re-layouts  20.1 us (22%)
    pallas_call x1, Pallas kernels, body(): pl.pallas_call(kernel, out_shape=(jax.ShapeDtypeStruct((512, 192), BF16),...  68.9 us
    unnamed x29, local copies, waits for them, and re-layouts  8.48 us
    pallas_call x2, local copies, waits for them, and re-layouts, body(): pl.pallas_call(kernel, out_shape=(jax.ShapeDtypeStruct((512, 192), BF16),...  2.55 us

profile of v1, /device:TPU:1, one launch (start us, length us, event | category | flops | bytes accessed | tf_op | source)
XLA Modules:
  0.0 89.8 jit_solution(17408568776393171309)
XLA Ops:
  0.6 1.3 %reshape.20 = bf16[192,4,192]{2,1,0:T(4,128)(2,1)S(1)} reshape(bf16[192,768]{1,0:T(8,128)(2,1)} %param.23) | data formatting | bytes 589824 | tf_op jit(solution)/shard_map/reshape | solution.py:467
  2.0 0.0 copy-start
  2.0 0.9 %copy-done = bf16[192,768]{1,0:T(8,128)(2,1)S(1)} copy-done((bf16[192,768]{1,0:T(8,128)(2,1)S(1)}, bf16[192,768]{1,0:T(8,128)(2,1)}, u32[]{:S(2)}) %copy-start) | copy-done | bytes 294936
  2.9 0.4 reshape.21
  3.4 0.1 pad_bitcast_fusion
  3.5 0.0 slice-start
  3.5 0.9 slice-done
  4.4 0.2 copy.43
  4.6 0.0 slice-start.1
  4.6 0.9 %slice-done.1 = bf16[768,128]{0,1:T(8,128)(2,1)S(1)} async-done(((bf16[768,192]{0,1:T(8,128)(2,1)}), bf16[768,128]{0,1:T(8,128)(2,1)S(1)}, s32[]{:S(2)}) %slice-start.1) | async-done | bytes 196632 | tf_op jit(solution)/shard_map/slice | solution.py:456
  5.5 0.2 copy.40
  5.7 0.0 slice-start.2
  5.7 0.9 %slice-done.2 = bf16[768,128]{0,1:T(8,128)(2,1)S(1)} async-done(((bf16[768,192]{0,1:T(8,128)(2,1)}), bf16[768,128]{0,1:T(8,128)(2,1)S(1)}, s32[]{:S(2)}) %slice-start.2) | async-done | bytes 196632 | tf_op jit(solution)/shard_map/slice | solution.py:457
  6.6 0.2 copy.41
  6.8 0.0 slice-start.4
  6.8 0.9 %slice-done.4 = bf16[768,128]{0,1:T(8,128)(2,1)S(1)} async-done(((bf16[768,192]{0,1:T(8,128)(2,1)}), bf16[768,128]{0,1:T(8,128)(2,1)S(1)}, s32[]{:S(2)}) %slice-start.4) | async-done | bytes 196632 | tf_op jit(solution)/shard_map/slice | solution.py:458
  7.7 0.2 copy.42
  7.9 0.0 slice-start.3
  7.9 0.9 slice-done.3
  8.8 0.2 copy.44
  9.0 0.0 slice-start.5
  9.0 0.9 slice-done.5
  9.9 0.2 copy.45
  10.0 0.0 copy-start.7
  10.0 0.5 concatenate.3.w_all
  10.5 0.5 copy-done.7
  11.0 0.0 copy-start.1
  11.0 0.9 %copy.33 = bf16[768,192]{1,0:T(8,128)(2,1)} copy(bf16[768,192]{0,1:T(8,128)(2,1)S(1)} %copy-done.7) | data formatting | bytes 589824 | tf_op args[11]
  11.9 0.0 copy-start.8
  11.9 1.1 %pad.16.w_cq = bf16[768,256]{1,0:T(8,128)(2,1)S(1)} pad(bf16[768,192]{1,0:T(8,128)(2,1)} %copy.33, bf16[]{:T(256)} %constant.2.clone.1), padding=0_0x0_64 | pad | bytes 688130 | tf_op jit(solution)/shard_map/jit(_pad)/pad | solution.py:465
  13.0 0.0 copy-done.8
  13.0 0.1 copy.36.parents
  13.1 0.0 copy-start.9
  13.1 0.7 copy-done.9
  13.7 0.1 copy.37.counts
  13.8 0.0 copy-start.6
  13.8 0.0 copy-done.1
  13.8 0.7 copy-done.6
  14.5 0.0 copy-start.3
  14.5 0.9 %copy-done.3 = s32[65536]{0:T(1024)S(1)} copy-done((s32[65536]{0:T(1024)S(1)}, s32[65536]{0:T(1024)}, u32[]{:S(2)}) %copy-start.3) | copy-done | bytes 262168
  15.4 0.0 copy-start.4
  15.4 0.8 copy-done.4
  16.2 0.0 copy-start.5
  16.2 0.8 copy-done.5
  17.0 68.9 %shard_map.148 = (bf16[512,192]{1,0:T(8,128)(2,1)S(1)}, bf16[32,192]{1,0:T(8,128)(2,1)S(1)}, bf16[512,192]{1,0:T(8,128)(2,1)S(1)}) custom-call(s32[8]{0:T(128)S(1)} %copy-done.6, bf16[512,768]{1,0:T(8,128)(2,1)S(1)} %copy-done.1, s32[512,128]{1,0:T(8,128)S(1)} %bitcast.6, bf16[32,768]{1,0:T(8,128)(2,1)S(1)} %copy-done.4, s32[32,16]{1,0:T(8,128)S(1)} %copy.36.parents, ...), custom_call_target="tpu_custom_call" | custom-call | tf_op jit(solution)/shard_map/pallas_call | solution.py:471
  86.0 0.0 copy-start.2
  86.0 0.7 copy-done.2
  86.7 1.8 %copy.38 = bf16[512,192]{0,1:T(8,128)(2,1)} copy(bf16[512,192]{1,0:T(8,128)(2,1)} %copy-done.2) | data formatting | bytes 393216 | tf_op jit(solution)/shard_map/pallas_call | solution.py:471
  88.4 0.8 copy.39
  89.2 0.6 copy.47
  (3 shorter events, 0.1 us)
Async XLA Ops:
  2.0 1.0 %copy-start = (bf16[192,768]{1,0:T(8,128)(2,1)S(1)}, bf16[192,768]{1,0:T(8,128)(2,1)}, u32[]{:S(2)}) copy-start(bf16[192,768]{1,0:T(8,128)(2,1)} %wco.1) | copy-start | bytes 884740
  3.5 0.9 slice-start
  4.6 0.9 %slice-start.1 = ((bf16[768,192]{0,1:T(8,128)(2,1)}), bf16[768,128]{0,1:T(8,128)(2,1)S(1)}, s32[]{:S(2)}) async-start(bf16[768,192]{0,1:T(8,128)(2,1)} %param.20), calls=%async_computation.1 | async-start | bytes 393216 | tf_op jit(solution)/shard_map/slice | solution.py:456
  5.7 0.9 %slice-start.2 = ((bf16[768,192]{0,1:T(8,128)(2,1)}), bf16[768,128]{0,1:T(8,128)(2,1)S(1)}, s32[]{:S(2)}) async-start(bf16[768,192]{0,1:T(8,128)(2,1)} %param.21), calls=%async_computation.2 | async-start | bytes 393216 | tf_op jit(solution)/shard_map/slice | solution.py:457
  6.8 0.9 %slice-start.4 = ((bf16[768,192]{0,1:T(8,128)(2,1)}), bf16[768,128]{0,1:T(8,128)(2,1)S(1)}, s32[]{:S(2)}) async-start(bf16[768,192]{0,1:T(8,128)(2,1)} %param.22), calls=%async_computation.4 | async-start | bytes 393216 | tf_op jit(solution)/shard_map/slice | solution.py:458
  7.9 0.9 %slice-start.3 = ((bf16[768,192]{0,1:T(8,128)(2,1)}), bf16[768,64]{0,1:T(8,128)(2,1)S(1)}, s32[]{:S(2)}) async-start(bf16[768,192]{0,1:T(8,128)(2,1)} %param.21), calls=%async_computation.3 | async-start | bytes 196608 | tf_op jit(solution)/shard_map/slice | solution.py:460
  9.0 0.9 %slice-start.5 = ((bf16[768,192]{0,1:T(8,128)(2,1)}), bf16[768,64]{0,1:T(8,128)(2,1)S(1)}, s32[]{:S(2)}) async-start(bf16[768,192]{0,1:T(8,128)(2,1)} %param.22), calls=%async_computation.5 | async-start | bytes 196608 | tf_op jit(solution)/shard_map/slice | solution.py:461
  10.0 1.0 %copy-start.7 = (bf16[768,192]{0,1:T(8,128)(2,1)S(1)}, bf16[768,192]{0,1:T(8,128)(2,1)}, u32[]{:S(2)}) copy-start(bf16[768,192]{0,1:T(8,128)(2,1)} %param.24) | copy-start | bytes 884740
  11.0 2.8 %copy-start.1 = (bf16[512,768]{1,0:T(8,128)(2,1)S(1)}, bf16[512,768]{1,0:T(8,128)(2,1)}, u32[]{:S(2)}) copy-start(bf16[512,768]{1,0:T(8,128)(2,1)} %tiles.1) | copy-start | bytes 2359300
  11.9 1.1 %copy-start.8 = (s32[32,16]{0,1:T(8,128)S(1)}, s32[32,16]{0,1:T(8,128)}, u32[]{:S(2)}) copy-start(s32[32,16]{0,1:T(8,128)} %param.17) | copy-start | bytes 6148
  13.1 0.7 copy-start.9
  13.8 0.7 copy-start.6
  14.5 0.9 %copy-start.3 = (s32[65536]{0:T(1024)S(1)}, s32[65536]{0:T(1024)}, u32[]{:S(2)}) copy-start(s32[65536]{0:T(1024)} %param.14) | copy-start | bytes 786436
  15.4 0.8 copy-start.4
  16.2 0.8 copy-start.5
  86.0 0.7 copy-start.2

commit v2 on v1

--- a/solution.py
+++ b/solution.py
@@ -46,14 +46,22 @@
     parents,
     counts,
     cotangent,
-    w_all,
-    w_cq,
-    wo4,
-    wco4,
+    wq_t,
+    wk_t,
+    wv_t,
+    wo,
+    wcq_t,
     wco,
     out_tile,
     out_region,
     out_grad,
+    tiles_in,
+    tissue_in,
+    w_t,
+    wo_in,
+    wcq_in,
+    wco_in,
+    wout,
     first,
     second,
     feats,
@@ -74,6 +82,8 @@
     rin,
     perm_a,
     perm_b,
+    rows_out,
+    loads,
     p1s,
     p1r,
     p2s,
@@ -121,6 +131,28 @@
         sent.append(copy)
         return copy
 
+    local = []
+
+    def load(src, dst):
+        copy = pltpu.make_async_copy(src, dst, loads.at[len(local)])
+        copy.start()
+        local.append(copy)
+        return copy
+
+    load_tiles = load(tiles, tiles_in)
+    load_w = [
+        load(wk_t.at[0:128], w_t.at[128:256]),
+        load(wv_t.at[0:128], w_t.at[256:384]),
+        load(wk_t.at[128:192], w_t.at[512:576]),
+        load(wv_t.at[128:192], w_t.at[576:640]),
+        load(wq_t.at[0:128], w_t.at[0:128]),
+        load(wq_t.at[128:192], w_t.at[384:448]),
+    ]
+    load_wo = load(wo, wo_in)
+    load_wcq = load(wcq_t, wcq_in.at[0:192])
+    load_wco = load(wco, wco_in)
+    load_tissue = load(tissue, tissue_in)
+
     barrier = pltpu.get_barrier_semaphore()
 
     def greet(seq, head):
@@ -151,18 +183,24 @@
                 x,
             )
         )
-    first[pl.ds(pl.multiple_of(q * 16, 16), 16), :] = tiles[
-        pl.ds(pl.multiple_of(x * 128 + q * 16, 16), 16), :
-    ]
+    load_wo.wait()
+    blocks_of(wo_in[...].astype(F32), wout)
     wcopies = []
     for d in range(1, NX):
         to = lax.rem(x + d, NX)
-        wcopies.append(go(wo4.at[to], wrecv.at[x], wos.at[d], wor.at[d], s, to))
-    wrecv[x] = wo4[x]
-
-    block = tiles[...]
-    ext[128:640, 0:256] = mm(block, w_all[:, 128:384]).astype(BF16)
-    ext[128:640, 256:384] = mm(block, w_all[:, 512:640]).astype(BF16)
+        wcopies.append(go(wout.at[to], wrecv.at[x], wos.at[d], wor.at[d], s, to))
+    wrecv[x] = wout[x]
+
+    load_tiles.wait()
+    for copy in load_w:
+        copy.wait()
+    w_t[448:512] = jnp.zeros((64, 768), BF16)
+    first[pl.ds(pl.multiple_of(q * 16, 16), 16), :] = tiles_in[
+        pl.ds(pl.multiple_of(x * 128 + q * 16, 16), 16), :
+    ]
+    block = tiles_in[...]
+    ext[128:640, 0:256] = nt(block, w_t[128:384]).astype(BF16)
+    ext[128:640, 256:384] = nt(block, w_t[512:640]).astype(BF16)
     halos = [
         go(ext.at[128:256], ext.at[640:768], has.at[0], har.at[0], before, x),
         go(ext.at[512:640], ext.at[0:128], has.at[1], har.at[1], after, x),
@@ -203,27 +241,28 @@
 
     low = iota((32, 128), 1) < HD
     rows32 = regions[...]
-    cq = (mm(rows32, w_cq[...]).astype(BF16)).astype(F32) * (HD**-0.5)
-    rk = mm(rows32, w_all[:, 128:384]).astype(BF16).astype(F32)
-    rkv2 = mm(rows32, w_all[:, 512:640]).astype(BF16).astype(F32)
+    load_wcq.wait()
+    load_wco.wait()
+    wcq_in[192:256] = jnp.zeros((64, 768), BF16)
+    cq = nt(rows32, wcq_in[...]).astype(BF16).astype(F32) * (HD**-0.5)
+    rk = nt(rows32, w_t[128:384]).astype(BF16).astype(F32)
+    rkv2 = nt(rows32, w_t[512:640]).astype(BF16).astype(F32)
     rk01, rv01 = rk[:, 0:128], rk[:, 128:256]
     cq0 = jnp.where(low, cq[:, 0:128], 0.0)
     cq1 = jnp.where(low, 0.0, cq[:, 0:128])
     cq2 = jnp.where(low, cq[:, 128:256], 0.0)
-    back = nt(cotangent[...], wco[...]).astype(BF16)
+    back_t = nt(wco_in[...], cotangent[...]).astype(BF16)
     place = iota((32, 768), 1)
     times = jnp.zeros((32, 768), F32)
     base = s * 512 - 128
-    count = counts[...]
-    lists = parents[...] - base
+    lists = jnp.where(iota((16, 32), 0) < counts[...], parents[...] - base, -1)
+    lists = jnp.transpose(lists.astype(F32)).astype(jnp.int32)
     for j in range(16):
-        hit = (lists[:, j : j + 1] == place) & (j < count)
-        times = times + jnp.where(hit, 1.0, 0.0)
+        times = times + jnp.where(lists[:, j : j + 1] == place, 1.0, 0.0)
     valid = times > 0.0
     for copy in halos:
         copy.wait_recv()
     outs = []
-    grads = []
     for h in range(3):
         query = (cq0, cq1, cq2)[h]
         own = jnp.sum(query * (rk01 if h < 2 else rkv2), axis=1, keepdims=True)
@@ -238,25 +277,17 @@
         weight_own = (ex_own / total).astype(BF16).astype(F32)
         mixed = (times * weight).astype(BF16)
         outs.append(mm(mixed, values) + weight_own * (rv01 if h < 2 else rkv2))
-        grads.append(tn(mixed, back[:, 0:128] if h < 2 else back[:, 128:192]))
+        grad = mm(back_t[64 * h : 64 * h + 64], mixed)
+        gown[64 * h : 64 * h + 64] = grad[:, 128:640]
+        gext[0, 64 * h : 64 * h + 64] = grad[:, 0:128].astype(BF16)
+        gext[1, 64 * h : 64 * h + 64] = grad[:, 640:768].astype(BF16)
     cross_a = jnp.where(low, outs[0], outs[1]).astype(BF16)
     cross_b = pltpu.roll(outs[2], 64, 1)[:, 0:64].astype(BF16)
-    low768 = iota((768, 128), 1) < HD
-    grad_a = jnp.where(low768, grads[0], grads[1])
-    grad_b = grads[2]
-    gown[:, 0:128] = grad_a[128:640]
-    gown[:, 128:192] = grad_b[128:640]
-    zero = jnp.zeros((128, 64), BF16)
-    gext[0:128, 0:128] = grad_a[0:128].astype(BF16)
-    gext[0:128, 128:256] = jnp.concatenate([grad_b[0:128].astype(BF16), zero], axis=1)
-    gext[128:256, 0:128] = grad_a[640:768].astype(BF16)
-    gext[128:256, 128:256] = jnp.concatenate([grad_b[640:768].astype(BF16), zero], axis=1)
     gcopies = [
-        go(gext.at[0:128], gnext, grs.at[0], grr.at[0], before, x),
-        go(gext.at[128:256], gprev, grs.at[1], grr.at[1], after, x),
+        go(gext.at[0], gnext, grs.at[0], grr.at[0], before, x),
+        go(gext.at[1], gprev, grs.at[1], grr.at[1], after, x),
     ]
-    for g in range(NX):
-        rout[g] = (mm(cross_a, wco4[g, 0:128]) + mm(cross_b, wco4[g, 128:192])).astype(BF16)
+    blocks_of(mm(cross_a, wco_in[0:128]) + mm(cross_b, wco_in[128:192]), rout)
     rcopies = []
     for d in range(1, NX):
         to = lax.rem(x + d, NX)
@@ -277,8 +308,9 @@
     wlast[:, 128:192] = jnp.zeros((NX, 64, 256), BF16)
 
     c = q * NZ + z
+    load_tissue.wait()
     pick = (iota((16, 128), 1) == c).astype(BF16)
-    tissue_n = nt(pick, tissue[...].astype(F32).astype(BF16)).astype(BF16)
+    tissue_n = nt(pick, tissue_in[...].astype(F32).astype(BF16)).astype(BF16)
     spread_n = (iota((512, 512), 0) == order_of(iota((512, 512), 1))).astype(BF16)
     tissue_row = mm(tissue_n, spread_n)[0:1]
     n_row = order_of(iota((1, 512), 1))
@@ -296,7 +328,7 @@
         left = part[:, 0].reshape(128, 384).astype(BF16)
         right = part[:, 1].reshape(128, 384).astype(BF16)
         qkv[128 * b : 128 * b + 128] = (
-            mm(left, w_all[0:384]) + mm(right, w_all[384:768])
+            nt(left, w_t[:, 0:384]) + nt(right, w_t[:, 384:768])
         ).astype(BF16)
 
     low128 = iota((128, 128), 1) < HD
@@ -355,9 +387,9 @@
 
     for copy in gcopies + rcopies:
         copy.wait_recv()
-    gown[0:128, 0:192] = gown[0:128, 0:192] + gprev[:, 0:192].astype(F32)
-    gown[384:512, 0:192] = gown[384:512, 0:192] + gnext[:, 0:192].astype(F32)
-    out_grad[...] = gown[:, 0:192].astype(BF16)
+    gown[:, 0:128] = gown[:, 0:128] + gprev[...].astype(F32)
+    gown[:, 384:512] = gown[:, 384:512] + gnext[...].astype(F32)
+    out_grad[...] = gown[...].astype(BF16)
     total = rin[0].astype(F32)
     for g in range(1, NX):
         total = total + rin[g].astype(F32)
@@ -385,13 +417,24 @@
         turned = pltpu.roll(half, 64, 1)
         for i in range(4):
             at = i * 128 + p * 16
-            out_tile[at : at + 16, 0:128] = pin[p, 16 * i : 16 * i + 16]
             k = (i & 1) * 16
-            out_tile[at : at + 16, 128:192] = (half if i < 2 else turned)[
-                k : k + 16, 0:64
-            ].astype(BF16)
+            rows_out[at : at + 16, 0:128] = pin[p, 16 * i : 16 * i + 16].astype(F32)
+            rows_out[at : at + 16, 128:256] = (half if i < 2 else turned)[k : k + 16]
+    for i in range(4):
+        at = i * 128
+        out_tile[0:128, at : at + 128] = jnp.transpose(rows_out[at : at + 128, 0:128]).astype(BF16)
+        out_tile[128:192, at : at + 128] = jnp.transpose(rows_out[at : at + 128, 128:256])[
+            0:64
+        ].astype(BF16)
     for copy in sent:
         copy.wait_send()
+
+
+def blocks_of(wide, out):
+    for g in range(NX):
+        at = g * 192 - (g & 1) * 64
+        piece = wide[:, at : at + 256]
+        out[g] = (pltpu.roll(piece, 192, 1) if g & 1 else piece).astype(BF16)
 
 
 def finish(acopies, j, own_chunk, att, wrecv, wlast, zout, low64):
@@ -450,35 +493,28 @@
     w_cross_query,
     w_cross_output,
 ):
-    pad = ((0, 0), (0, 64))
-    w_all = jnp.concatenate(
-        [
-            w_query[:, :128],
-            w_key[:, :128],
-            w_value[:, :128],
-            jnp.pad(w_query[:, 128:], pad),
-            w_key[:, 128:],
-            w_value[:, 128:],
-        ],
-        axis=1,
-    )
-    w_cq = jnp.pad(w_cross_query, pad)
-    split = lambda w: jnp.transpose(
-        jnp.pad(w.reshape(192, NX, 192), ((0, 0), (0, 0), (0, 64))), (1, 0, 2)
-    )
     dma = pltpu.SemaphoreType.DMA
     vmem = lambda *shape: pltpu.VMEM(shape, BF16)
-    return pl.pallas_call(
+    tile_t, region, grad_t = pl.pallas_call(
         kernel,
         out_shape=(
-            jax.ShapeDtypeStruct((512, 192), BF16),
+            jax.ShapeDtypeStruct((192, 512), BF16),
             jax.ShapeDtypeStruct((32, 192), BF16),
-            jax.ShapeDtypeStruct((512, 192), BF16),
+            jax.ShapeDtypeStruct((192, 512), BF16),
         ),
         in_specs=[pl.BlockSpec(memory_space=pltpu.SMEM)]
-        + [pl.BlockSpec(memory_space=pltpu.VMEM)] * 11,
+        + [pl.BlockSpec(memory_space=pl.ANY)] * 2
+        + [pl.BlockSpec(memory_space=pltpu.VMEM)] * 4
+        + [pl.BlockSpec(memory_space=pl.ANY)] * 6,
         out_specs=(pl.BlockSpec(memory_space=pltpu.VMEM),) * 3,
         scratch_shapes=[
+            vmem(512, 768),
+            pltpu.VMEM((512, 128), jnp.int32),
+            vmem(640, 768),
+            vmem(192, 768),
+            vmem(256, 768),
+            vmem(192, 768),
+            vmem(4, 192, 256),
             vmem(128, 768),
             vmem(16, 16, 384),
             vmem(16, 4, 16, 384),
@@ -491,14 +527,16 @@
             vmem(16, 48, 128),
             vmem(8, 96, 128),
             vmem(8, 96, 128),
-            vmem(256, 256),
-            pltpu.VMEM((512, 256), F32),
-            vmem(128, 256),
-            vmem(128, 256),
+            vmem(2, 192, 128),
+            pltpu.VMEM((192, 512), F32),
+            vmem(192, 128),
+            vmem(192, 128),
             vmem(4, 32, 256),
             vmem(4, 32, 256),
             vmem(512, 512),
             vmem(256, 256),
+            pltpu.VMEM((512, 256), F32),
+            dma((12,)),
             dma((8,)),
             dma((8,)),
             dma((16,)),
@@ -521,22 +559,24 @@
             dma((4,)),
         ],
         compiler_params=pltpu.CompilerParams(
-            collective_id=0, has_side_effects=True, vmem_limit_bytes=48 * 1024 * 1024
+            collective_id=0, has_side_effects=True, vmem_limit_bytes=60 * 1024 * 1024
         ),
     )(
         slide_lengths,
         tile_rows,
         tissue_mask.reshape(512, 128),
         region_rows,
-        parent_lists,
-        child_counts.reshape(32, 1),
+        parent_lists.T,
+        child_counts.reshape(1, 32),
         region_cotangent,
-        w_all,
-        w_cq,
-        split(w_output),
-        split(w_cross_output),
+        w_query.T,
+        w_key.T,
+        w_value.T,
+        w_output,
+        w_cross_query.T,
         w_cross_output,
     )
+    return tile_t.T, region, grad_t.T
 
 
 def solution(mesh):

time: 90.4 us -> 74.5 us (0.82)
  local copies, waits for them, and re-layouts: 20.1 us -> 2.95 us
  Pallas kernels: 68.9 us -> 70.7 us
    unnamed x29 -> x7, local copies, waits for them, and re-layouts: 8.48 us -> 2.95 us
    slice x12 -> x0, local copies, waits for them, and re-layouts: 5.45 us -> none  [the longest x2 0.93 us: body(): w_key[:, :128]]
    pallas_call x2 -> x0, local copies, waits for them, and re-layouts: 2.55 us -> none  [body(): pl.pallas_call(kernel, out_shape=(jax.ShapeDtypeStruct((512, 192), BF16),...]
    reshape x5 -> x0, local copies, waits for them, and re-layouts: 1.86 us -> none  [the longest x4 1.78 us: body(): w.reshape(192, NX, 192)]
    pallas_call x1, Pallas kernels: 68.9 us -> 70.7 us  [body(): pl.pallas_call(kernel, out_shape=(jax.ShapeDtypeStruct((192, 512), BF16),...]
    pad x2 -> x0, local copies, waits for them, and re-layouts: 1.11 us -> none  [the longest x1 1.07 us: body(): w_cq = jnp.pad(w_cross_query, pad)]
where the time goes in v2:
time: 74.5 us; the launch traced here: 74.3 us
  Pallas kernels  70.7 us (95%)
  local copies, waits for them, and re-layouts  2.95 us (4%)
    pallas_call x1, Pallas kernels, body(): pl.pallas_call(kernel, out_shape=(jax.ShapeDtypeStruct((192, 512), BF16),...  70.7 us
    unnamed x7, local copies, waits for them, and re-layouts  2.95 us

profile of v2, /device:TPU:1, one launch (start us, length us, event | category | flops | bytes accessed | tf_op | source)
XLA Modules:
  0.0 74.3 jit_solution(4884542269789561813)
XLA Ops:
  0.6 70.7 %shard_map.148 = (bf16[192,512]{1,0:T(8,128)(2,1)}, bf16[32,192]{1,0:T(8,128)(2,1)}, bf16[192,512]{1,0:T(8,128)(2,1)}) custom-call(s32[8]{0:T(128)} %lengths.1, bf16[512,768]{1,0:T(8,128)(2,1)} %tiles.1, s32[512,128]{1,0:T(8,128)} %bitcast.13, bf16[32,768]{1,0:T(8,128)(2,1)} %regions.1, s32[16,32]{1,0:T(8,128)} %bitcast.16, s32[1,32]{1,0:T(1,128)} %bitcast.17, ...), custom_call_target="tpu_custom_call" | custom-call | tf_op jit(solution)/shard_map/pallas_call | solution.py:498
  71.4 0.0 copy-start.1
  71.4 0.0 copy-start
  71.4 1.7 %copy.19 = bf16[512,192]{0,1:T(8,128)(2,1)} copy(bf16[512,192]{0,1:T(8,128)(2,1)} %bitcast.15) | data formatting | bytes 393216
  73.0 0.0 copy-done.1
  73.0 0.6 copy.20
  73.6 0.0 copy-done
  73.7 0.7 copy.21
Async XLA Ops:
  71.4 1.7 %copy-start.1 = (bf16[32,192]{1,0:T(8,128)(2,1)S(1)}, bf16[32,192]{1,0:T(8,128)(2,1)}, u32[]{:S(2)}) copy-start(bf16[32,192]{1,0:T(8,128)(2,1)} %get-tuple-element.13) | copy-start | bytes 36868
  71.4 2.3 %copy-start = (bf16[192,512]{1,0:T(8,128)(2,1)S(1)}, bf16[192,512]{1,0:T(8,128)(2,1)}, u32[]{:S(2)}) copy-start(bf16[192,512]{1,0:T(8,128)(2,1)} %get-tuple-element.8) | copy-start | bytes 589828

commit v3 on v2

--- a/solution.py
+++ b/solution.py
@@ -57,6 +57,11 @@
     out_grad,
     tiles_in,
     tissue_in,
+    regions_in,
+    parents_in,
+    counts_in,
+    cot_in,
+    lens,
     w_t,
     wo_in,
     wcq_in,
@@ -131,28 +136,6 @@
         sent.append(copy)
         return copy
 
-    local = []
-
-    def load(src, dst):
-        copy = pltpu.make_async_copy(src, dst, loads.at[len(local)])
-        copy.start()
-        local.append(copy)
-        return copy
-
-    load_tiles = load(tiles, tiles_in)
-    load_w = [
-        load(wk_t.at[0:128], w_t.at[128:256]),
-        load(wv_t.at[0:128], w_t.at[256:384]),
-        load(wk_t.at[128:192], w_t.at[512:576]),
-        load(wv_t.at[128:192], w_t.at[576:640]),
-        load(wq_t.at[0:128], w_t.at[0:128]),
-        load(wq_t.at[128:192], w_t.at[384:448]),
-    ]
-    load_wo = load(wo, wo_in)
-    load_wcq = load(wcq_t, wcq_in.at[0:192])
-    load_wco = load(wco, wco_in)
-    load_tissue = load(tissue, tissue_in)
-
     barrier = pltpu.get_barrier_semaphore()
 
     def greet(seq, head):
@@ -183,6 +166,35 @@
                 x,
             )
         )
+    local = []
+
+    def load(src, dst):
+        copy = pltpu.make_async_copy(src, dst, loads.at[len(local)])
+        copy.start()
+        local.append(copy)
+        return copy
+
+    load_tiles = load(tiles, tiles_in)
+    load_w = [
+        load(wk_t.at[0:128], w_t.at[128:256]),
+        load(wv_t.at[0:128], w_t.at[256:384]),
+        load(wk_t.at[128:192], w_t.at[512:576]),
+        load(wv_t.at[128:192], w_t.at[576:640]),
+        load(wq_t.at[0:128], w_t.at[0:128]),
+        load(wq_t.at[128:192], w_t.at[384:448]),
+    ]
+    load_wo = load(wo, wo_in)
+    load_wcq = load(wcq_t, wcq_in.at[0:192])
+    load_wco = load(wco, wco_in)
+    load_regions = [
+        load(regions, regions_in),
+        load(parents, parents_in),
+        load(counts, counts_in),
+        load(cotangent, cot_in),
+    ]
+    load_mask = [load(tissue, tissue_in), load(lengths, lens)]
+
+
     load_wo.wait()
     blocks_of(wo_in[...].astype(F32), wout)
     wcopies = []
@@ -209,12 +221,12 @@
     lane = iota((256, 128), 1)
     row = iota((256, 128), 0)
     source = (lane & 15) * 16 + (lane >> 4)
-    left = (source == row).astype(BF16)
-    right = (source + 8 == row).astype(BF16)
+    turn0 = (source == row).astype(BF16)
+    turn1 = (source + 8 == row).astype(BF16)
     for copy in hop1:
         copy.wait_recv()
     second[...] = (
-        (mm(left, first[:, 0:384]) + mm(right, first[:, 384:768]))
+        (mm(turn0, first[:, 0:384]) + mm(turn1, first[:, 384:768]))
         .astype(BF16)
         .reshape(NZ, 16, 384)
     )
@@ -224,25 +236,39 @@
         hop2[d] = go(second.at[to], feats.at[z, x], p2s.at[d], p2r.at[d], to * NQ + q, x)
     feats[z, x] = second[z]
 
-    hopx = []
-
-    def spread(d):
-        at = lax.rem(z - d + NZ, NZ)
-        for e in range(1, NX):
-            to = lax.rem(x + e, NX)
-            hopx.append(
-                go(feats.at[at, x], feats.at[at, x], pxs.at[e, d], pxr.at[e, d], s, to)
-            )
+    right = lax.rem(x + 1, NX)
+    left = lax.rem(x + 3, NX)
+    hopx = {}
+    steps = (0,) + ZORDER
+
+    def place_of(k):
+        return lax.rem(z - steps[k] + NZ, NZ)
+
+    def spread(k):
+        at = place_of(k)
+        part = feats.at[at, x]
+        hopx[0, k] = go(part, part, pxs.at[0, k], pxr.at[0, k], s, right)
+        hopx[1, k] = go(part, part, pxs.at[1, k], pxr.at[1, k], s, left)
+
+    def relay(k):
+        hopx.pop((k % 2, k)).wait_recv()
+        part = feats.at[place_of(k), right if k % 2 else left]
+        hopx[2, k] = go(part, part, pxs.at[2, k], pxr.at[2, k], s, left if k % 2 else right)
+
+    def arrive(k):
+        hop2[steps[k]].wait_recv()
+        spread(k)
+        if k >= 2:
+            relay(k - 2)
 
     spread(0)
-    for d in ZORDER:
-        hop2[d].wait_recv()
-        spread(d)
 
     low = iota((32, 128), 1) < HD
-    rows32 = regions[...]
     load_wcq.wait()
     load_wco.wait()
+    for copy in load_regions:
+        copy.wait()
+    rows32 = regions_in[...]
     wcq_in[192:256] = jnp.zeros((64, 768), BF16)
     cq = nt(rows32, wcq_in[...]).astype(BF16).astype(F32) * (HD**-0.5)
     rk = nt(rows32, w_t[128:384]).astype(BF16).astype(F32)
@@ -251,11 +277,11 @@
     cq0 = jnp.where(low, cq[:, 0:128], 0.0)
     cq1 = jnp.where(low, 0.0, cq[:, 0:128])
     cq2 = jnp.where(low, cq[:, 128:256], 0.0)
-    back_t = nt(wco_in[...], cotangent[...]).astype(BF16)
+    back_t = nt(wco_in[...], cot_in[...]).astype(BF16)
     place = iota((32, 768), 1)
     times = jnp.zeros((32, 768), F32)
     base = s * 512 - 128
-    lists = jnp.where(iota((16, 32), 0) < counts[...], parents[...] - base, -1)
+    lists = jnp.where(iota((16, 32), 0) < counts_in[...], parents_in[...] - base, -1)
     lists = jnp.transpose(lists.astype(F32)).astype(jnp.int32)
     for j in range(16):
         times = times + jnp.where(lists[:, j : j + 1] == place, 1.0, 0.0)
@@ -294,6 +320,9 @@
         rcopies.append(go(rout.at[to], rin.at[x], res.at[d], rer.at[d], s, to))
     rin[x] = rout[x]
 
+    for k in range(1, 8):
+        arrive(k)
+
     prow = iota((512, 512), 0)
     pcol = iota((512, 512), 1)
     perm_a[...] = (
@@ -308,7 +337,8 @@
     wlast[:, 128:192] = jnp.zeros((NX, 64, 256), BF16)
 
     c = q * NZ + z
-    load_tissue.wait()
+    for copy in load_mask:
+        copy.wait()
     pick = (iota((16, 128), 1) == c).astype(BF16)
     tissue_n = nt(pick, tissue_in[...].astype(F32).astype(BF16)).astype(BF16)
     spread_n = (iota((512, 512), 0) == order_of(iota((512, 512), 1))).astype(BF16)
@@ -317,43 +347,77 @@
     slide_row = jnp.zeros((1, 512), jnp.int32)
     end = jnp.int32(0)
     for k in range(8):
-        end = end + lengths[k]
+        end = end + lens[k]
         slide_row = slide_row + jnp.where(n_row * 128 + c >= end, 1, 0)
 
-    for copy in hopx:
-        copy.wait_recv()
+    for k in range(8, 16):
+        arrive(k)
+    relay(14)
+    relay(15)
+    w_out_rows(wcopies, wrecv, wlast)
 
     for b in range(4):
-        part = feats[4 * b : 4 * b + 4].astype(F32).reshape(16, 2, 8, 384)
-        left = part[:, 0].reshape(128, 384).astype(BF16)
-        right = part[:, 1].reshape(128, 384).astype(BF16)
-        qkv[128 * b : 128 * b + 128] = (
-            nt(left, w_t[:, 0:384]) + nt(right, w_t[:, 384:768])
-        ).astype(BF16)
+        group = range(4 * b, 4 * b + 4)
+        for k in group:
+            for e in range(3):
+                if (e, k) in hopx:
+                    hopx[e, k].wait_recv()
+        part = jnp.stack([feats[place_of(k)] for k in group]).astype(F32)
+        part = part.reshape(16, 2, 8, 384)
+        upper = part[:, 0].reshape(128, 384).astype(BF16)
+        lower = part[:, 1].reshape(128, 384).astype(BF16)
+        made = nt(upper, w_t[:, 0:384]) + nt(lower, w_t[:, 384:768])
+        made = made.astype(BF16).reshape(4, 32, 640)
+        for i in range(4):
+            qkv[place_of(group[i])] = made[i]
+    every = qkv[...].reshape(512, 640)
 
     low128 = iota((128, 128), 1) < HD
-    keys01 = qkv[:, 128:256].astype(F32)
+    keys01 = every[:, 128:256].astype(F32)
     low512 = iota((512, 128), 1) < HD
     key0 = jnp.where(low512, keys01, 0.0).astype(BF16)
     key1 = jnp.where(low512, 0.0, keys01).astype(BF16)
-    key_value2 = qkv[:, 512:640]
-    values01 = qkv[:, 256:384]
+    key_value2 = every[:, 512:640]
+    values01 = every[:, 256:384]
     has_tissue = tissue_row > 0.5
     own_chunk = z // 4
     low64 = iota((64, 128), 1) < HD
 
     acopies = {}
+    zcopies = []
+    chunks = [lax.rem(own_chunk + k, 4) for k in (2, 1, 3, 0)]
+
+    def pass_on(j):
+        acopies.pop((0, j)).wait_recv()
+        part = att.at[left, chunks[j], 0:96]
+        acopies[2, j] = go(part, part, axs.at[2, j], axr.at[2, j], s, right)
+        acopies.pop((1, j)).wait_recv()
+        part = att.at[right, chunks[j], 96:192]
+        acopies[3, j] = go(part, part, axs.at[3, j], axr.at[3, j], s, left)
+
+    def finish(j):
+        acopies[2, j].wait_recv()
+        acopies[3, j].wait_recv()
+        output_rows(chunks[j], att, wrecv, wlast, zout, low64)
+        for k in range(4):
+            if (j, k) != (3, 0):
+                to = chunks[j] * 4 + lax.rem(z + k, 4)
+                zcopies.append(
+                    go(zout.at[to], zin.at[z], zas.at[j, k], zar.at[j, k], to * NQ + q, x)
+                )
+
     for j in range(4):
-        chunk = lax.rem(own_chunk + j, 4)
+        chunk = chunks[j]
         at = pl.multiple_of(chunk * 128, 128)
-        query01 = (qkv[pl.ds(at, 128), 0:128].astype(F32) * (HD**-0.5)).astype(BF16)
-        query2 = (qkv[pl.ds(at, 128), 384:512].astype(F32) * (HD**-0.5)).astype(BF16)
+        query = qkv[pl.ds(chunk * 4, 4)].reshape(128, 640)
+        query01 = (query[:, 0:128].astype(F32) * (HD**-0.5)).astype(BF16)
+        query2 = (query[:, 384:512].astype(F32) * (HD**-0.5)).astype(BF16)
         row = iota((128, 1), 0) + at
         n_mine = order_of(row)
         slide_mine = jnp.zeros((128, 1), jnp.int32)
         end = jnp.int32(0)
         for k in range(8):
-            end = end + lengths[k]
+            end = end + lens[k]
             slide_mine = slide_mine + jnp.where(n_mine * 128 + c >= end, 1, 0)
         base_ok = (slide_mine == slide_row) & (has_tissue | (row == iota((128, 512), 1)))
         parts = []
@@ -369,20 +433,16 @@
         att[x, chunk, 128:192] = jnp.where(
             low64, pltpu.roll(parts[2][0:64], 64, 1), parts[2][64:128]
         ).astype(BF16)
-        for e in range(1, NX):
-            to = lax.rem(x + e, NX)
-            acopies[e, j] = go(
-                att.at[x, chunk], att.at[x, chunk], axs.at[e, j], axr.at[e, j], s, to
-            )
-        if j == 0:
-            for copy in wcopies:
-                copy.wait_recv()
-            wlast[:, 64:128] = wrecv[:, 128:192]
-        if j > 0:
-            finish(acopies, j - 1, own_chunk, att, wrecv, wlast, zout, low64)
-            send_z(go, zout, zin, zas, zar, own_chunk, j - 1, z, q, x)
-    finish(acopies, 3, own_chunk, att, wrecv, wlast, zout, low64)
-    send_z(go, zout, zin, zas, zar, own_chunk, 3, z, q, x)
+        part = att.at[x, chunk]
+        acopies[0, j] = go(part, part, axs.at[0, j], axr.at[0, j], s, right)
+        acopies[1, j] = go(part, part, axs.at[1, j], axr.at[1, j], s, left)
+        if j >= 1:
+            pass_on(j - 1)
+        if j >= 2:
+            finish(j - 2)
+    pass_on(3)
+    finish(2)
+    finish(3)
     zin[z] = zout[z]
 
     for copy in gcopies + rcopies:
@@ -395,12 +455,8 @@
         total = total + rin[g].astype(F32)
     out_region[...] = total[:, 0:192].astype(BF16)
 
-    for d in range(1, NZ):
-        copy = remote(
-            zout.at[z], zin.at[z], zas.at[d], zar.at[d], lax.rem(z + d, NZ) * NQ + q, x
-        )
+    for copy in zcopies:
         copy.wait_recv()
-        sent.append(copy)
     rows_a = mm(perm_a[...], zin[:, 0:32].reshape(512, 128)).astype(BF16)
     rows_b = mm(perm_b[...], zin[:, 32:48].reshape(256, 128)).astype(BF16)
     pout[:, 0:64] = rows_a.reshape(NQ, 64, 128)
@@ -437,10 +493,13 @@
         out[g] = (pltpu.roll(piece, 192, 1) if g & 1 else piece).astype(BF16)
 
 
-def finish(acopies, j, own_chunk, att, wrecv, wlast, zout, low64):
-    for e in range(1, NX):
-        acopies[e, j].wait_recv()
-    chunk = lax.rem(own_chunk + j, 4)
+def w_out_rows(wcopies, wrecv, wlast):
+    for copy in wcopies:
+        copy.wait_recv()
+    wlast[:, 64:128] = wrecv[:, 128:192]
+
+
+def output_rows(chunk, att, wrecv, wlast, zout, low64):
     acc = jnp.zeros((128, 256), F32)
     upper = jnp.zeros((64, 256), F32)
     lower = jnp.zeros((64, 256), F32)
@@ -458,24 +517,6 @@
     at = chunk * 4
     zout[pl.ds(at, 4), 0:32] = acc[:, 0:128].reshape(4, 32, 128).astype(BF16)
     zout[pl.ds(at, 4), 32:48] = packed.reshape(4, 16, 128).astype(BF16)
-
-
-def send_z(go, zout, zin, zas, zar, own_chunk, j, z, q, x):
-    for k in range(4):
-        to = lax.rem(own_chunk + j, 4) * 4 + k
-        d = lax.rem(to - z + NZ, NZ)
-
-        @pl.when(d != 0)
-        def _():
-            copy = pltpu.make_async_remote_copy(
-                src_ref=zout.at[to],
-                dst_ref=zin.at[z],
-                send_sem=zas.at[d],
-                recv_sem=zar.at[d],
-                device_id={"seq": to * NQ + q, "head": x},
-                device_id_type=MESH,
-            )
-            copy.start()
 
 
 def body(
@@ -502,14 +543,16 @@
             jax.ShapeDtypeStruct((32, 192), BF16),
             jax.ShapeDtypeStruct((192, 512), BF16),
         ),
-        in_specs=[pl.BlockSpec(memory_space=pltpu.SMEM)]
-        + [pl.BlockSpec(memory_space=pl.ANY)] * 2
-        + [pl.BlockSpec(memory_space=pltpu.VMEM)] * 4
-        + [pl.BlockSpec(memory_space=pl.ANY)] * 6,
+        in_specs=[pl.BlockSpec(memory_space=pl.ANY)] * 13,
         out_specs=(pl.BlockSpec(memory_space=pltpu.VMEM),) * 3,
         scratch_shapes=[
             vmem(512, 768),
             pltpu.VMEM((512, 128), jnp.int32),
+            vmem(32, 768),
+            pltpu.VMEM((16, 32), jnp.int32),
+            pltpu.VMEM((1, 32), jnp.int32),
+            vmem(32, 768),
+            pltpu.SMEM((8,), jnp.int32),
             vmem(640, 768),
             vmem(192, 768),
             vmem(256, 768),
@@ -518,7 +561,7 @@
             vmem(128, 768),
             vmem(16, 16, 384),
             vmem(16, 4, 16, 384),
-            vmem(512, 640),
+            vmem(16, 32, 640),
             vmem(768, 384),
             vmem(4, 192, 256),
             vmem(4, 192, 256),
@@ -536,7 +579,7 @@
             vmem(512, 512),
             vmem(256, 256),
             pltpu.VMEM((512, 256), F32),
-            dma((12,)),
+            dma((16,)),
             dma((8,)),
             dma((8,)),
             dma((16,)),
@@ -549,8 +592,8 @@
             dma((2,)),
             dma((4, 4)),
             dma((4, 4)),
-            dma((16,)),
-            dma((16,)),
+            dma((4, 4)),
+            dma((4, 4)),
             dma((8,)),
             dma((8,)),
             dma((2,)),

time: 74.5 us -> 79.1 us (1.062)
  Pallas kernels: 70.7 us -> 75.3 us
    pallas_call x1, Pallas kernels: 70.7 us -> 75.3 us  [body(): pl.pallas_call(kernel, out_shape=(jax.ShapeDtypeStruct((192, 512), BF16),...]
where the time goes in v3:
time: 79.1 us; the launch traced here: 78.9 us
  Pallas kernels  75.3 us (95%)
  local copies, waits for them, and re-layouts  2.95 us (4%)
    pallas_call x1, Pallas kernels, body(): pl.pallas_call(kernel, out_shape=(jax.ShapeDtypeStruct((192, 512), BF16),...  75.3 us
    unnamed x7, local copies, waits for them, and re-layouts  2.95 us

profile of v3, /device:TPU:1, one launch (start us, length us, event | category | flops | bytes accessed | tf_op | source)
XLA Modules:
  0.0 78.9 jit_solution(13219696682188055367)
XLA Ops:
  0.6 75.3 %shard_map.148 = (bf16[192,512]{1,0:T(8,128)(2,1)}, bf16[32,192]{1,0:T(8,128)(2,1)}, bf16[192,512]{1,0:T(8,128)(2,1)}) custom-call(s32[8]{0:T(128)} %lengths.1, bf16[512,768]{1,0:T(8,128)(2,1)} %tiles.1, s32[512,128]{1,0:T(8,128)} %bitcast.13, bf16[32,768]{1,0:T(8,128)(2,1)} %regions.1, s32[16,32]{1,0:T(8,128)} %bitcast.16, s32[1,32]{1,0:T(1,128)} %bitcast.17, ...), custom_call_target="tpu_custom_call" | custom-call | tf_op jit(solution)/shard_map/pallas_call | solution.py:539
  75.9 0.0 copy-start.1
  75.9 0.0 copy-start
  75.9 1.7 %copy.19 = bf16[512,192]{0,1:T(8,128)(2,1)} copy(bf16[512,192]{0,1:T(8,128)(2,1)} %bitcast.15) | data formatting | bytes 393216
  77.6 0.0 copy-done.1
  77.6 0.6 copy.20
  78.2 0.0 copy-done
  78.2 0.7 copy.21
Async XLA Ops:
  75.9 1.7 %copy-start.1 = (bf16[32,192]{1,0:T(8,128)(2,1)S(1)}, bf16[32,192]{1,0:T(8,128)(2,1)}, u32[]{:S(2)}) copy-start(bf16[32,192]{1,0:T(8,128)(2,1)} %get-tuple-element.13) | copy-start | bytes 36868
  75.9 2.3 %copy-start = (bf16[192,512]{1,0:T(8,128)(2,1)S(1)}, bf16[192,512]{1,0:T(8,128)(2,1)}, u32[]{:S(2)}) copy-start(bf16[192,512]{1,0:T(8,128)(2,1)} %get-tuple-element.8) | copy-start | bytes 589828

commit v4 on v3

--- a/solution.py
+++ b/solution.py
@@ -34,8 +34,11 @@
     return jnp.dot(a, b, preferred_element_type=F32)
 
 
-def order_of(row):
-    return (row & ~31) | ((row & 7) << 2) | ((row >> 3) & 3)
+def order_of(row, z):
+    k = row >> 5
+    near = (k + 1) >> 1
+    zk = (z + jnp.where((k & 1) == 1, -near, near)) & (NZ - 1)
+    return (zk << 5) | ((row & 7) << 2) | ((row >> 3) & 3)
 
 
 def kernel(
@@ -230,38 +233,42 @@
         .astype(BF16)
         .reshape(NZ, 16, 384)
     )
+    steps = (0,) + ZORDER
     hop2 = {}
-    for d in ZORDER:
-        to = lax.rem(z + d, NZ)
-        hop2[d] = go(second.at[to], feats.at[z, x], p2s.at[d], p2r.at[d], to * NQ + q, x)
-    feats[z, x] = second[z]
+    for k in range(1, NZ):
+        to = lax.rem(z + steps[k], NZ)
+        hop2[k] = go(second.at[to], feats.at[x, k], p2s.at[k], p2r.at[k], to * NQ + q, x)
+    feats[x, 0] = second[z]
 
     right = lax.rem(x + 1, NX)
     left = lax.rem(x + 3, NX)
     hopx = {}
-    steps = (0,) + ZORDER
-
-    def place_of(k):
-        return lax.rem(z - steps[k] + NZ, NZ)
-
-    def spread(k):
-        at = place_of(k)
-        part = feats.at[at, x]
-        hopx[0, k] = go(part, part, pxs.at[0, k], pxr.at[0, k], s, right)
-        hopx[1, k] = go(part, part, pxs.at[1, k], pxr.at[1, k], s, left)
-
-    def relay(k):
-        hopx.pop((k % 2, k)).wait_recv()
-        part = feats.at[place_of(k), right if k % 2 else left]
-        hopx[2, k] = go(part, part, pxs.at[2, k], pxr.at[2, k], s, left if k % 2 else right)
-
-    def arrive(k):
-        hop2[steps[k]].wait_recv()
-        spread(k)
-        if k >= 2:
-            relay(k - 2)
-
-    spread(0)
+
+    def spread(b):
+        for k in range(4 * b, 4 * b + 4):
+            if k:
+                hop2[k].wait_recv()
+        part = feats.at[x, 4 * b : 4 * b + 4]
+        hopx[0, b] = go(part, part, pxs.at[0, b], pxr.at[0, b], s, right)
+        hopx[1, b] = go(part, part, pxs.at[1, b], pxr.at[1, b], s, left)
+
+    def relay(b):
+        hopx[0, b].wait_recv()
+        part = feats.at[left, 4 * b : 4 * b + 2]
+        hopx[2, b] = go(part, part, pxs.at[2, b], pxr.at[2, b], s, right)
+        hopx[1, b].wait_recv()
+        part = feats.at[right, 4 * b + 2 : 4 * b + 4]
+        hopx[3, b] = go(part, part, pxs.at[3, b], pxr.at[3, b], s, left)
+
+    def project(b):
+        hopx[2, b].wait_recv()
+        hopx[3, b].wait_recv()
+        part = [feats[i, k].astype(F32) for k in range(4 * b, 4 * b + 4) for i in range(NX)]
+        upper = jnp.concatenate([p[0:8] for p in part], axis=0).astype(BF16)
+        lower = jnp.concatenate([p[8:16] for p in part], axis=0).astype(BF16)
+        qkv[128 * b : 128 * b + 128] = (
+            nt(upper, w_t[:, 0:384]) + nt(lower, w_t[:, 384:768])
+        ).astype(BF16)
 
     low = iota((32, 128), 1) < HD
     load_wcq.wait()
@@ -320,8 +327,7 @@
         rcopies.append(go(rout.at[to], rin.at[x], res.at[d], rer.at[d], s, to))
     rin[x] = rout[x]
 
-    for k in range(1, 8):
-        arrive(k)
+    spread(0)
 
     prow = iota((512, 512), 0)
     pcol = iota((512, 512), 1)
@@ -341,36 +347,28 @@
         copy.wait()
     pick = (iota((16, 128), 1) == c).astype(BF16)
     tissue_n = nt(pick, tissue_in[...].astype(F32).astype(BF16)).astype(BF16)
-    spread_n = (iota((512, 512), 0) == order_of(iota((512, 512), 1))).astype(BF16)
+    spread_n = (iota((512, 512), 0) == order_of(iota((512, 512), 1), z)).astype(BF16)
     tissue_row = mm(tissue_n, spread_n)[0:1]
-    n_row = order_of(iota((1, 512), 1))
+    n_row = order_of(iota((1, 512), 1), z)
     slide_row = jnp.zeros((1, 512), jnp.int32)
     end = jnp.int32(0)
     for k in range(8):
         end = end + lens[k]
         slide_row = slide_row + jnp.where(n_row * 128 + c >= end, 1, 0)
 
-    for k in range(8, 16):
-        arrive(k)
-    relay(14)
-    relay(15)
+    spread(1)
+    relay(0)
     w_out_rows(wcopies, wrecv, wlast)
-
-    for b in range(4):
-        group = range(4 * b, 4 * b + 4)
-        for k in group:
-            for e in range(3):
-                if (e, k) in hopx:
-                    hopx[e, k].wait_recv()
-        part = jnp.stack([feats[place_of(k)] for k in group]).astype(F32)
-        part = part.reshape(16, 2, 8, 384)
-        upper = part[:, 0].reshape(128, 384).astype(BF16)
-        lower = part[:, 1].reshape(128, 384).astype(BF16)
-        made = nt(upper, w_t[:, 0:384]) + nt(lower, w_t[:, 384:768])
-        made = made.astype(BF16).reshape(4, 32, 640)
-        for i in range(4):
-            qkv[place_of(group[i])] = made[i]
-    every = qkv[...].reshape(512, 640)
+    spread(2)
+    relay(1)
+    project(0)
+    spread(3)
+    relay(2)
+    project(1)
+    relay(3)
+    project(2)
+    project(3)
+    every = qkv[...]
 
     low128 = iota((128, 128), 1) < HD
     keys01 = every[:, 128:256].astype(F32)
@@ -380,12 +378,11 @@
     key_value2 = every[:, 512:640]
     values01 = every[:, 256:384]
     has_tissue = tissue_row > 0.5
-    own_chunk = z // 4
     low64 = iota((64, 128), 1) < HD
 
     acopies = {}
     zcopies = []
-    chunks = [lax.rem(own_chunk + k, 4) for k in (2, 1, 3, 0)]
+    chunks = (3, 2, 1, 0)
 
     def pass_on(j):
         acopies.pop((0, j)).wait_recv()
@@ -399,21 +396,21 @@
         acopies[2, j].wait_recv()
         acopies[3, j].wait_recv()
         output_rows(chunks[j], att, wrecv, wlast, zout, low64)
-        for k in range(4):
-            if (j, k) != (3, 0):
-                to = chunks[j] * 4 + lax.rem(z + k, 4)
+        for k in range(4 * chunks[j], 4 * chunks[j] + 4):
+            if k:
+                to = lax.rem(z - steps[k] + NZ, NZ)
                 zcopies.append(
-                    go(zout.at[to], zin.at[z], zas.at[j, k], zar.at[j, k], to * NQ + q, x)
+                    go(zout.at[k], zin.at[z], zas.at[k], zar.at[k], to * NQ + q, x)
                 )
 
     for j in range(4):
         chunk = chunks[j]
-        at = pl.multiple_of(chunk * 128, 128)
-        query = qkv[pl.ds(chunk * 4, 4)].reshape(128, 640)
+        at = chunk * 128
+        query = qkv[at : at + 128]
         query01 = (query[:, 0:128].astype(F32) * (HD**-0.5)).astype(BF16)
         query2 = (query[:, 384:512].astype(F32) * (HD**-0.5)).astype(BF16)
         row = iota((128, 1), 0) + at
-        n_mine = order_of(row)
+        n_mine = order_of(row, z)
         slide_mine = jnp.zeros((128, 1), jnp.int32)
         end = jnp.int32(0)
         for k in range(8):
@@ -436,14 +433,15 @@
         part = att.at[x, chunk]
         acopies[0, j] = go(part, part, axs.at[0, j], axr.at[0, j], s, right)
         acopies[1, j] = go(part, part, axs.at[1, j], axr.at[1, j], s, left)
-        if j >= 1:
-            pass_on(j - 1)
         if j >= 2:
-            finish(j - 2)
+            pass_on(j - 2)
+    finish(0)
+    pass_on(2)
+    finish(1)
     pass_on(3)
     finish(2)
     finish(3)
-    zin[z] = zout[z]
+    zin[z] = zout[0]
 
     for copy in gcopies + rcopies:
         copy.wait_recv()
@@ -515,8 +513,8 @@
         pltpu.roll(two[:, 1].reshape(64, 128), 64, 1),
     )
     at = chunk * 4
-    zout[pl.ds(at, 4), 0:32] = acc[:, 0:128].reshape(4, 32, 128).astype(BF16)
-    zout[pl.ds(at, 4), 32:48] = packed.reshape(4, 16, 128).astype(BF16)
+    zout[at : at + 4, 0:32] = acc[:, 0:128].reshape(4, 32, 128).astype(BF16)
+    zout[at : at + 4, 32:48] = packed.reshape(4, 16, 128).astype(BF16)
 
 
 def body(
@@ -560,8 +558,8 @@
             vmem(4, 192, 256),
             vmem(128, 768),
             vmem(16, 16, 384),
-            vmem(16, 4, 16, 384),
-            vmem(16, 32, 640),
+            vmem(4, 16, 16, 384),
+            vmem(512, 640),
             vmem(768, 384),
             vmem(4, 192, 256),
             vmem(4, 192, 256),
@@ -584,16 +582,16 @@
             dma((8,)),
             dma((16,)),
             dma((16,)),
-            dma((4, 16)),
-            dma((4, 16)),
+            dma((4, 4)),
+            dma((4, 4)),
             dma((4,)),
             dma((4,)),
             dma((2,)),
             dma((2,)),
             dma((4, 4)),
             dma((4, 4)),
-            dma((4, 4)),
-            dma((4, 4)),
+            dma((16,)),
+            dma((16,)),
             dma((8,)),
             dma((8,)),
             dma((2,)),

time: 79.1 us -> 73.3 us (0.927)
  Pallas kernels: 75.3 us -> 69.5 us
    pallas_call x1, Pallas kernels: 75.3 us -> 69.5 us  [body(): pl.pallas_call(kernel, out_shape=(jax.ShapeDtypeStruct((192, 512), BF16),...]
where the time goes in v4:
time: 73.3 us; the launch traced here: 73.1 us
  Pallas kernels  69.5 us (95%)
  local copies, waits for them, and re-layouts  2.95 us (4%)
    pallas_call x1, Pallas kernels, body(): pl.pallas_call(kernel, out_shape=(jax.ShapeDtypeStruct((192, 512), BF16),...  69.5 us
    unnamed x7, local copies, waits for them, and re-layouts  2.95 us

profile of v4, /device:TPU:1, one launch (start us, length us, event | category | flops | bytes accessed | tf_op | source)
XLA Modules:
  0.0 73.1 jit_solution(10104939559236850916)
XLA Ops:
  0.6 69.5 %shard_map.148 = (bf16[192,512]{1,0:T(8,128)(2,1)}, bf16[32,192]{1,0:T(8,128)(2,1)}, bf16[192,512]{1,0:T(8,128)(2,1)}) custom-call(s32[8]{0:T(128)} %lengths.1, bf16[512,768]{1,0:T(8,128)(2,1)} %tiles.1, s32[512,128]{1,0:T(8,128)} %bitcast.13, bf16[32,768]{1,0:T(8,128)(2,1)} %regions.1, s32[16,32]{1,0:T(8,128)} %bitcast.16, s32[1,32]{1,0:T(1,128)} %bitcast.17, ...), custom_call_target="tpu_custom_call" | custom-call | tf_op jit(solution)/shard_map/pallas_call | solution.py:537
  70.1 0.0 copy-start.1
  70.1 0.0 copy-start
  70.1 1.7 %copy.19 = bf16[512,192]{0,1:T(8,128)(2,1)} copy(bf16[512,192]{0,1:T(8,128)(2,1)} %bitcast.15) | data formatting | bytes 393216
  71.8 0.0 copy-done.1
  71.8 0.6 copy.20
  72.4 0.0 copy-done
  72.4 0.7 copy.21
Async XLA Ops:
  70.1 1.7 %copy-start.1 = (bf16[32,192]{1,0:T(8,128)(2,1)S(1)}, bf16[32,192]{1,0:T(8,128)(2,1)}, u32[]{:S(2)}) copy-start(bf16[32,192]{1,0:T(8,128)(2,1)} %get-tuple-element.13) | copy-start | bytes 36868
  70.1 2.3 %copy-start = (bf16[192,512]{1,0:T(8,128)(2,1)S(1)}, bf16[192,512]{1,0:T(8,128)(2,1)}, u32[]{:S(2)}) copy-start(bf16[192,512]{1,0:T(8,128)(2,1)} %get-tuple-element.8) | copy-start | bytes 589828

commit v5 on v4

--- a/solution.py
+++ b/solution.py
@@ -240,29 +240,22 @@
         hop2[k] = go(second.at[to], feats.at[x, k], p2s.at[k], p2r.at[k], to * NQ + q, x)
     feats[x, 0] = second[z]
 
-    right = lax.rem(x + 1, NX)
-    left = lax.rem(x + 3, NX)
+    peers = [lax.rem(x + e, NX) for e in (1, 3, 2)]
     hopx = {}
 
     def spread(b):
-        for k in range(4 * b, 4 * b + 4):
-            if k:
-                hop2[k].wait_recv()
-        part = feats.at[x, 4 * b : 4 * b + 4]
-        hopx[0, b] = go(part, part, pxs.at[0, b], pxr.at[0, b], s, right)
-        hopx[1, b] = go(part, part, pxs.at[1, b], pxr.at[1, b], s, left)
-
-    def relay(b):
-        hopx[0, b].wait_recv()
-        part = feats.at[left, 4 * b : 4 * b + 2]
-        hopx[2, b] = go(part, part, pxs.at[2, b], pxr.at[2, b], s, right)
-        hopx[1, b].wait_recv()
-        part = feats.at[right, 4 * b + 2 : 4 * b + 4]
-        hopx[3, b] = go(part, part, pxs.at[3, b], pxr.at[3, b], s, left)
+        for b in (2 * b, 2 * b + 1):
+            for k in range(2 * b, 2 * b + 2):
+                if k:
+                    hop2[k].wait_recv()
+            part = feats.at[x, 2 * b : 2 * b + 2]
+            for e, to in enumerate(peers):
+                hopx[e, b] = go(part, part, pxs.at[e, b], pxr.at[e, b], s, to)
 
     def project(b):
-        hopx[2, b].wait_recv()
-        hopx[3, b].wait_recv()
+        for e in range(3):
+            hopx[e, 2 * b].wait_recv()
+            hopx[e, 2 * b + 1].wait_recv()
         part = [feats[i, k].astype(F32) for k in range(4 * b, 4 * b + 4) for i in range(NX)]
         upper = jnp.concatenate([p[0:8] for p in part], axis=0).astype(BF16)
         lower = jnp.concatenate([p[8:16] for p in part], axis=0).astype(BF16)
@@ -357,15 +350,11 @@
         slide_row = slide_row + jnp.where(n_row * 128 + c >= end, 1, 0)
 
     spread(1)
-    relay(0)
     w_out_rows(wcopies, wrecv, wlast)
     spread(2)
-    relay(1)
     project(0)
     spread(3)
-    relay(2)
     project(1)
-    relay(3)
     project(2)
     project(3)
     every = qkv[...]
@@ -384,17 +373,9 @@
     zcopies = []
     chunks = (3, 2, 1, 0)
 
-    def pass_on(j):
-        acopies.pop((0, j)).wait_recv()
-        part = att.at[left, chunks[j], 0:96]
-        acopies[2, j] = go(part, part, axs.at[2, j], axr.at[2, j], s, right)
-        acopies.pop((1, j)).wait_recv()
-        part = att.at[right, chunks[j], 96:192]
-        acopies[3, j] = go(part, part, axs.at[3, j], axr.at[3, j], s, left)
-
     def finish(j):
-        acopies[2, j].wait_recv()
-        acopies[3, j].wait_recv()
+        for e in range(3):
+            acopies[e, j].wait_recv()
         output_rows(chunks[j], att, wrecv, wlast, zout, low64)
         for k in range(4 * chunks[j], 4 * chunks[j] + 4):
             if k:
@@ -431,14 +412,10 @@
             low64, pltpu.roll(parts[2][0:64], 64, 1), parts[2][64:128]
         ).astype(BF16)
         part = att.at[x, chunk]
-        acopies[0, j] = go(part, part, axs.at[0, j], axr.at[0, j], s, right)
-        acopies[1, j] = go(part, part, axs.at[1, j], axr.at[1, j], s, left)
-        if j >= 2:
-            pass_on(j - 2)
+        for e, to in enumerate(peers):
+            acopies[e, j] = go(part, part, axs.at[e, j], axr.at[e, j], s, to)
     finish(0)
-    pass_on(2)
     finish(1)
-    pass_on(3)
     finish(2)
     finish(3)
     zin[z] = zout[0]
@@ -582,8 +559,8 @@
             dma((8,)),
             dma((16,)),
             dma((16,)),
-            dma((4, 4)),
-            dma((4, 4)),
+            dma((4, 8)),
+            dma((4, 8)),
             dma((4,)),
             dma((4,)),
             dma((2,)),

time: 73.3 us -> 66.8 us (0.911)
  Pallas kernels: 69.5 us -> 63 us
    pallas_call x1, Pallas kernels: 69.5 us -> 63 us  [body(): pl.pallas_call(kernel, out_shape=(jax.ShapeDtypeStruct((192, 512), BF16),...]
where the time goes in v5:
time: 66.8 us; the launch traced here: 66.6 us
  Pallas kernels  63 us (94%)
  local copies, waits for them, and re-layouts  2.95 us (4%)
    pallas_call x1, Pallas kernels, body(): pl.pallas_call(kernel, out_shape=(jax.ShapeDtypeStruct((192, 512), BF16),...  63 us
    unnamed x7, local copies, waits for them, and re-layouts  2.95 us

profile of v5, /device:TPU:1, one launch (start us, length us, event | category | flops | bytes accessed | tf_op | source)
XLA Modules:
  0.0 66.6 jit_solution(15512697124411152064)
XLA Ops:
  0.6 63.0 %shard_map.148 = (bf16[192,512]{1,0:T(8,128)(2,1)}, bf16[32,192]{1,0:T(8,128)(2,1)}, bf16[192,512]{1,0:T(8,128)(2,1)}) custom-call(s32[8]{0:T(128)} %lengths.1, bf16[512,768]{1,0:T(8,128)(2,1)} %tiles.1, s32[512,128]{1,0:T(8,128)} %bitcast.13, bf16[32,768]{1,0:T(8,128)(2,1)} %regions.1, s32[16,32]{1,0:T(8,128)} %bitcast.16, s32[1,32]{1,0:T(1,128)} %bitcast.17, ...), custom_call_target="tpu_custom_call" | custom-call | tf_op jit(solution)/shard_map/pallas_call | solution.py:514
  63.7 0.0 copy-start.1
  63.7 0.0 copy-start
  63.7 1.7 %copy.19 = bf16[512,192]{0,1:T(8,128)(2,1)} copy(bf16[512,192]{0,1:T(8,128)(2,1)} %bitcast.15) | data formatting | bytes 393216
  65.4 0.0 copy-done.1
  65.4 0.6 copy.20
  66.0 0.0 copy-done
  66.0 0.7 %copy.21 = bf16[512,192]{0,1:T(8,128)(2,1)} copy(bf16[512,192]{0,1:T(8,128)(2,1)S(1)} %bitcast.14) | data formatting | bytes 393216
Async XLA Ops:
  63.7 1.7 %copy-start.1 = (bf16[32,192]{1,0:T(8,128)(2,1)S(1)}, bf16[32,192]{1,0:T(8,128)(2,1)}, u32[]{:S(2)}) copy-start(bf16[32,192]{1,0:T(8,128)(2,1)} %get-tuple-element.13) | copy-start | bytes 36868
  63.7 2.3 %copy-start = (bf16[192,512]{1,0:T(8,128)(2,1)S(1)}, bf16[192,512]{1,0:T(8,128)(2,1)}, u32[]{:S(2)}) copy-start(bf16[192,512]{1,0:T(8,128)(2,1)} %get-tuple-element.8) | copy-start | bytes 589828

commit v6 on v5

--- a/solution.py
+++ b/solution.py
@@ -55,7 +55,7 @@
     wo,
     wcq_t,
     wco,
-    out_tile,
+    pin,
     out_region,
     out_grad,
     tiles_in,
@@ -81,7 +81,8 @@
     zout,
     zin,
     pout,
-    pin,
+    rfin,
+    gfin,
     gext,
     gown,
     gprev,
@@ -90,7 +91,7 @@
     rin,
     perm_a,
     perm_b,
-    rows_out,
+    osem,
     loads,
     p1s,
     p1r,
@@ -424,11 +425,17 @@
         copy.wait_recv()
     gown[:, 0:128] = gown[:, 0:128] + gprev[...].astype(F32)
     gown[:, 384:512] = gown[:, 384:512] + gnext[...].astype(F32)
-    out_grad[...] = gown[...].astype(BF16)
+    gfin[...] = gown[...].astype(BF16)
     total = rin[0].astype(F32)
     for g in range(1, NX):
         total = total + rin[g].astype(F32)
-    out_region[...] = total[:, 0:192].astype(BF16)
+    rfin[...] = total[:, 0:192].astype(BF16)
+    outward = [
+        pltpu.make_async_copy(rfin, out_region, osem.at[1]),
+        pltpu.make_async_copy(gfin, out_grad, osem.at[2]),
+    ]
+    for copy in outward:
+        copy.start()
 
     for copy in zcopies:
         copy.wait_recv()
@@ -440,23 +447,13 @@
     for d in range(1, NQ):
         to = lax.rem(q + d, NQ)
         backs.append(go(pout.at[to], pin.at[q], pbs.at[d], pbr.at[d], z * NQ + to, x))
-    pin[q] = pout[q]
+    own_back = pltpu.make_async_copy(pout.at[q], pin.at[q], osem.at[0])
+    own_back.start()
     for copy in backs:
         copy.wait_recv()
-    for p in range(NQ):
-        half = pin[p, 64:96].astype(F32)
-        turned = pltpu.roll(half, 64, 1)
-        for i in range(4):
-            at = i * 128 + p * 16
-            k = (i & 1) * 16
-            rows_out[at : at + 16, 0:128] = pin[p, 16 * i : 16 * i + 16].astype(F32)
-            rows_out[at : at + 16, 128:256] = (half if i < 2 else turned)[k : k + 16]
-    for i in range(4):
-        at = i * 128
-        out_tile[0:128, at : at + 128] = jnp.transpose(rows_out[at : at + 128, 0:128]).astype(BF16)
-        out_tile[128:192, at : at + 128] = jnp.transpose(rows_out[at : at + 128, 128:256])[
-            0:64
-        ].astype(BF16)
+    own_back.wait()
+    for copy in outward:
+        copy.wait()
     for copy in sent:
         copy.wait_send()
 
@@ -494,6 +491,25 @@
     zout[at : at + 4, 32:48] = packed.reshape(4, 16, 128).astype(BF16)
 
 
+def assemble(pin, region, grad, out_tile, out_region, out_grad, rows_out):
+    out_region[...] = region[...]
+    out_grad[...] = grad[...]
+    for p in range(NQ):
+        half = pin[p, 64:96].astype(F32)
+        turned = pltpu.roll(half, 64, 1)
+        for i in range(4):
+            at = i * 128 + p * 16
+            k = (i & 1) * 16
+            rows_out[at : at + 16, 0:128] = pin[p, 16 * i : 16 * i + 16].astype(F32)
+            rows_out[at : at + 16, 128:256] = (half if i < 2 else turned)[k : k + 16]
+    for i in range(4):
+        at = i * 128
+        out_tile[0:128, at : at + 128] = jnp.transpose(rows_out[at : at + 128, 0:128]).astype(BF16)
+        out_tile[128:192, at : at + 128] = jnp.transpose(rows_out[at : at + 128, 128:256])[
+            0:64
+        ].astype(BF16)
+
+
 def body(
     tile_rows,
     tissue_mask,
@@ -511,15 +527,15 @@
 ):
     dma = pltpu.SemaphoreType.DMA
     vmem = lambda *shape: pltpu.VMEM(shape, BF16)
-    tile_t, region, grad_t = pl.pallas_call(
+    parts, region, grad_t = pl.pallas_call(
         kernel,
         out_shape=(
-            jax.ShapeDtypeStruct((192, 512), BF16),
+            jax.ShapeDtypeStruct((8, 96, 128), BF16),
             jax.ShapeDtypeStruct((32, 192), BF16),
             jax.ShapeDtypeStruct((192, 512), BF16),
         ),
         in_specs=[pl.BlockSpec(memory_space=pl.ANY)] * 13,
-        out_specs=(pl.BlockSpec(memory_space=pltpu.VMEM),) * 3,
+        out_specs=(pl.BlockSpec(memory_space=pl.ANY),) * 3,
         scratch_shapes=[
             vmem(512, 768),
             pltpu.VMEM((512, 128), jnp.int32),
@@ -544,7 +560,8 @@
             vmem(16, 48, 128),
             vmem(16, 48, 128),
             vmem(8, 96, 128),
-            vmem(8, 96, 128),
+            vmem(32, 192),
+            vmem(192, 512),
             vmem(2, 192, 128),
             pltpu.VMEM((192, 512), F32),
             vmem(192, 128),
@@ -553,7 +570,7 @@
             vmem(4, 32, 256),
             vmem(512, 512),
             vmem(256, 256),
-            pltpu.VMEM((512, 256), F32),
+            dma((3,)),
             dma((16,)),
             dma((8,)),
             dma((8,)),
@@ -594,6 +611,15 @@
         w_cross_query.T,
         w_cross_output,
     )
+    tile_t, region, grad_t = pl.pallas_call(
+        assemble,
+        out_shape=(
+            jax.ShapeDtypeStruct((192, 512), BF16),
+            jax.ShapeDtypeStruct((32, 192), BF16),
+            jax.ShapeDtypeStruct((192, 512), BF16),
+        ),
+        scratch_shapes=[pltpu.VMEM((512, 256), F32)],
+    )(parts, region, grad_t)
     return tile_t.T, region, grad_t.T
 
 

time: 66.8 us -> 64.9 us (0.972)
  local copies, waits for them, and re-layouts: 2.95 us -> 0 us
  Pallas kernels: 63 us -> 64.1 us
    unnamed x7 -> x0, local copies, waits for them, and re-layouts: 2.95 us -> none
    pallas_call x1 -> x2, Pallas kernels: 63 us -> 64.1 us  [the longest x1 62.2 us: body(): pl.pallas_call(kernel, out_shape=(jax.ShapeDtypeStruct((8, 96, 128), BF16...]
where the time goes in v6:
time: 64.9 us; the launch traced here: 64.7 us
  Pallas kernels  64.1 us (99%)
    pallas_call x1, Pallas kernels, body(): pl.pallas_call(kernel, out_shape=(jax.ShapeDtypeStruct((8, 96, 128), BF16...  62.2 us
    pallas_call x1, Pallas kernels, body(): pl.pallas_call(assemble, out_shape=(jax.ShapeDtypeStruct((192, 512), BF16...  1.89 us

profile of v6, /device:TPU:1, one launch (start us, length us, event | category | flops | bytes accessed | tf_op | source)
XLA Modules:
  0.0 64.7 jit_solution(7067207816437220340)
XLA Ops:
  0.6 62.2 %shard_map.148 = (bf16[8,96,128]{2,1,0:T(8,128)(2,1)}, bf16[32,192]{1,0:T(8,128)(2,1)}, bf16[192,512]{1,0:T(8,128)(2,1)}) custom-call(s32[8]{0:T(128)} %lengths.1, bf16[512,768]{1,0:T(8,128)(2,1)} %tiles.1, s32[512,128]{1,0:T(8,128)} %bitcast.13, bf16[32,768]{1,0:T(8,128)(2,1)} %regions.1, s32[16,32]{1,0:T(8,128)} %bitcast.14, s32[1,32]{1,0:T(1,128)} %bitcast.15, ...), custom_call_target="tpu_custom_call" | custom-call | tf_op jit(solution)/shard_map/pallas_call | solution.py:530
  62.8 1.9 %shard_map.149 = (bf16[192,512]{1,0:T(8,128)(2,1)}, bf16[32,192]{1,0:T(8,128)(2,1)}, bf16[192,512]{1,0:T(8,128)(2,1)}) custom-call(bf16[8,96,128]{2,1,0:T(8,128)(2,1)} %get-tuple-element.9.pin, bf16[32,192]{1,0:T(8,128)(2,1)} %get-tuple-element.10.region, bf16[192,512]{1,0:T(8,128)(2,1)} %get-tuple-element.11.grad), custom_call_target="tpu_custom_call" | custom-call | tf_op jit(solution)/shard_map/pallas_call | solution.py:614

commit v7 on v6

--- a/solution.py
+++ b/solution.py
@@ -147,14 +147,14 @@
             barrier, inc=1, device_id={"seq": seq, "head": head}, device_id_type=MESH
         )
 
+    for d in reversed(ZORDER):
+        greet(lax.rem(z + d, NZ) * NQ + q, x)
+    greet(after, x)
+    greet(before, x)
     for d in range(1, NQ):
         greet(z * NQ + lax.rem(q + d, NQ), x)
-    for d in ZORDER:
-        greet(lax.rem(z + d, NZ) * NQ + q, x)
     for d in range(1, NX):
         greet(s, lax.rem(x + d, NX))
-    greet(after, x)
-    greet(before, x)
     pl.semaphore_wait(barrier, (NQ - 1) + (NZ - 1) + (NX - 1) + 2)
 
     hop1 = []

time: 64.9 us -> 64.8 us (level)
  no operation moved by 1% of the time
where the time goes in v7:
time: 64.8 us; the launch traced here: 64.4 us
  Pallas kernels  63.7 us (98%)
    pallas_call x1, Pallas kernels, body(): pl.pallas_call(kernel, out_shape=(jax.ShapeDtypeStruct((8, 96, 128), BF16...  61.8 us
    pallas_call x1, Pallas kernels, body(): pl.pallas_call(assemble, out_shape=(jax.ShapeDtypeStruct((192, 512), BF16...  1.89 us

profile of v7, /device:TPU:1, one launch (start us, length us, event | category | flops | bytes accessed | tf_op | source)
XLA Modules:
  0.0 64.4 jit_solution(15045229126188550743)
XLA Ops:
  0.6 61.8 %shard_map.148 = (bf16[8,96,128]{2,1,0:T(8,128)(2,1)}, bf16[32,192]{1,0:T(8,128)(2,1)}, bf16[192,512]{1,0:T(8,128)(2,1)}) custom-call(s32[8]{0:T(128)} %lengths.1, bf16[512,768]{1,0:T(8,128)(2,1)} %tiles.1, s32[512,128]{1,0:T(8,128)} %bitcast.13, bf16[32,768]{1,0:T(8,128)(2,1)} %regions.1, s32[16,32]{1,0:T(8,128)} %bitcast.14, s32[1,32]{1,0:T(1,128)} %bitcast.15, ...), custom_call_target="tpu_custom_call" | custom-call | tf_op jit(solution)/shard_map/pallas_call | solution.py:530
  62.5 1.9 %shard_map.149 = (bf16[192,512]{1,0:T(8,128)(2,1)}, bf16[32,192]{1,0:T(8,128)(2,1)}, bf16[192,512]{1,0:T(8,128)(2,1)}) custom-call(bf16[8,96,128]{2,1,0:T(8,128)(2,1)} %get-tuple-element.9.pin, bf16[32,192]{1,0:T(8,128)(2,1)} %get-tuple-element.10.region, bf16[192,512]{1,0:T(8,128)(2,1)} %get-tuple-element.11.grad), custom_call_target="tpu_custom_call" | custom-call | tf_op jit(solution)/shard_map/pallas_call | solution.py:614
